TPU v7x, 32 devices: a whole 2x2x4 slice. The times are simulated.
32 devices in a mesh: tun: 8 (over y, x, core), sec: 4 (over z).
Axes of the slice: x: 2, y: 2, z: 4, core: 2. Of those that a mesh axis runs over, the one named last changes fastest.
Arguments:
- wind_vector: float32 [3, 64, 64, 128], P(None, 'tun', 'sec'), may hold values from -3 to 3
- thermal_surplus: float32 [64, 64, 128], P('tun', 'sec'), may hold values from -4 to 4
- carbon_particulate: float32 [64, 64, 128], P('tun', 'sec'), may hold values from 0 to 1
- particle_bin_weight: float32 [16, 64, 64, 128], P(None, 'tun', 'sec'), may hold values from 0 to 1
- particle_bin_tally: int32 [64, 64, 128], P('tun', 'sec'), may hold values from 0 to 16
- spray_region_label: int32 [64, 64, 128], P('tun', 'sec'), may hold values from 0 to 8
- nozzle_onset_step: int32 [8], replicated, may hold values from 0 to 2
Outputs:
- velocity_out: float32 [3, 64, 64, 128], P(None, 'tun', 'sec')
- temperature_out: float32 [64, 64, 128], P('tun', 'sec')
- soot_out: float32 [64, 64, 128], P('tun', 'sec')
- mass_out: float32 [16, 64, 64, 128], P(None, 'tun', 'sec')
- count_out: int32 [64, 64, 128], P('tun', 'sec')
Inputs may be any that keep to these rules, and one draw needn't show every extreme that they name: A cell's live slots are its first particle_bin_tally slots.
All inputs are finite; a program needn't handle non-finite values.
Results may differ from a plain program's by a relative error of at most 0.0003.
Values sent between devices are 32-bit elements; how exact they have to be, the bound alone decides.
A program may use at most 64 MiB of HBM per device.

v0:
```python
import jax
import jax.numpy as jnp
from jax import lax
from jax.sharding import PartitionSpec as P

visc_base = 0.2
time_step = 0.1
buoyancy = 0.5
drag_rate = 0.3
vent_speed = 1.0
inject_rate = 0.5
evap_rate = 0.4
latent_heat = 0.5
scavenge = 0.3


def extended(cells, sides, width):
    for axis, dim in sides:
        count = lax.axis_size(axis)
        ends = count - 1
        head = lax.slice_in_dim(cells, 0, width, axis=dim)
        tail = lax.slice_in_dim(cells, cells.shape[dim] - width, cells.shape[dim], axis=dim)
        cells = jnp.concatenate(
            [
                lax.ppermute(tail, axis, [(i, (i + 1) % count) for i in range(ends)]),
                cells,
                lax.ppermute(head, axis, [((i + 1) % count, i) for i in range(ends)]),
            ],
            axis=dim,
        )
    return cells


def passed_along(block, axis, distance):
    devices = range(lax.axis_size(axis))
    route = [(i - distance, i) for i in devices if i - distance in devices]
    return lax.ppermute(block, axis, route)


def neighbour(array, dim, offset):
    result = array
    lead = array.ndim - 3
    for split_axis in range(3):
        full = array.shape[lead + split_axis]
        start = 1 + offset if split_axis == dim else 1
        result = lax.slice_in_dim(result, start, start + full - 2, axis=lead + split_axis)
    return result


def advance(padded):
    centre = neighbour(padded, 0, 0)
    viscous = visc_base * (1.0 + 0.5 * jnp.tanh(padded[3]))
    visc_centre = neighbour(viscous, 0, 0)
    diffusion = jnp.zeros_like(centre)
    advection = jnp.zeros_like(centre)
    for dim in range(3):
        upper = neighbour(padded, dim, 1)
        lower = neighbour(padded, dim, -1)
        diffusion = diffusion + 0.5 * (visc_centre + neighbour(viscous, dim, 1)) * (upper - centre)
        diffusion = diffusion + 0.5 * (visc_centre + neighbour(viscous, dim, -1)) * (lower - centre)
        advection = advection + 0.5 * centre[dim] * (upper - lower)
    fresh = centre + time_step * (diffusion - advection)
    along = fresh[0] + time_step * drag_rate * (vent_speed - centre[0])
    upward = fresh[2] + time_step * buoyancy * centre[3]
    return jnp.stack([along, fresh[1], upward, fresh[3], fresh[4]])


def mist(transport_state, mass, count, spray_region_label, nozzle_onset_step, substep):
    slots = jnp.arange(mass.shape[0], dtype=jnp.int32)
    live = (slots[:, None, None, None] < count[None]).astype(jnp.float32)
    zones = jnp.arange(1, nozzle_onset_step.shape[0] + 1, dtype=jnp.int32)
    spraying = (nozzle_onset_step <= substep).astype(jnp.float32)
    zone_hit = (spray_region_label[None] == zones[:, None, None, None]).astype(jnp.float32)
    active = jnp.sum(zone_hit * spraying[:, None, None, None], axis=0)
    mass = mass + inject_rate * live * active[None]
    loaded = jnp.sum(live * mass, axis=0)
    evaporated = evap_rate * live * mass * jax.nn.sigmoid(transport_state[3])[None]
    heat = transport_state[3] - latent_heat * jnp.sum(evaporated, axis=0)
    sooty = transport_state[4] / (1.0 + scavenge * loaded)
    transport_state = jnp.stack(
        [transport_state[0], transport_state[1], transport_state[2], heat, sooty]
    )
    return (transport_state, mass - evaporated)


def local(
    wind_vector,
    thermal_surplus,
    carbon_particulate,
    particle_bin_weight,
    particle_bin_tally,
    spray_region_label,
    nozzle_onset_step,
):
    transport_state = jnp.concatenate(
        [wind_vector, thermal_surplus[None], carbon_particulate[None]], axis=0
    )
    mass, count = (particle_bin_weight, particle_bin_tally)
    slot_total = mass.shape[0]
    for substep in range(2):
        moving = extended(transport_state[0:3], (("tun", 1), ("sec", 2)), 1)
        heated = extended(transport_state[3], (("tun", 0), ("sec", 1)), 1)
        smoke = extended(transport_state[4], (("tun", 0), ("sec", 1)), 1)
        padded = jnp.concatenate([moving, heated[None], smoke[None]], axis=0)
        outgoing = jnp.concatenate([mass[:, -1], count[-1][None].astype(jnp.float32)], axis=0)
        incoming = passed_along(outgoing, "tun", 1)
        padded = jnp.pad(padded, ((0, 0), (0, 0), (0, 0), (1, 1)))
        transport_state = advance(padded)
        mass = jnp.concatenate([incoming[:slot_total][:, None], mass[:, :-1]], axis=1)
        count = jnp.concatenate([incoming[slot_total][None].astype(jnp.int32), count[:-1]], axis=0)
        transport_state, mass = mist(
            transport_state, mass, count, spray_region_label, nozzle_onset_step, substep
        )
    return (transport_state[0:3], transport_state[3], transport_state[4], mass, count)


def solution(mesh):
    return jax.shard_map(
        local,
        mesh=mesh,
        in_specs=(
            P(None, "tun", "sec", None),
            P("tun", "sec", None),
            P("tun", "sec", None),
            P(None, "tun", "sec", None),
            P("tun", "sec", None),
            P("tun", "sec", None),
            P(),
        ),
        out_specs=(
            P(None, "tun", "sec", None),
            P("tun", "sec", None),
            P("tun", "sec", None),
            P(None, "tun", "sec", None),
            P("tun", "sec", None),
        ),
        check_vma=False,
    )
```

profile of v0, /device:TPU:12, one launch (start us, length us, event | category | flops | bytes accessed | tf_op | source)
XLA Modules:
  0.0 96.3 jit_solution(1629149012874971075)
XLA Ops:
  1.4 2.8 %collective-permute-start.9 = (f32[1,16,128]{2,1,0:T(8,128)S(1)}, f32[1,16,128]{2,1,0:T(8,128)S(1)}, u32[]{:S(2)}, u32[]{:S(2)}) collective-permute-start(f32[1,16,128]{2,1,0:T(8,128)S(1)} %get-tuple-element.81), channel_id=1, source_target_pairs={{4,0},{8,4},{12,8},{16,12},{20,16},{24,20},{28,24},{5,1},{9,5},{13... | collective-permute-start | bytes 24584 | tf_op jit(solution)/shard_map/ppermute | solution.py:27
  4.2 1.9 %collective-permute-start.8 = (f32[1,16,128]{2,1,0:T(8,128)S(1)}, f32[1,16,128]{2,1,0:T(8,128)S(1)}, u32[]{:S(2)}, u32[]{:S(2)}) collective-permute-start(f32[1,16,128]{2,1,0:T(8,128)S(1)} %get-tuple-element.82), channel_id=1, source_target_pairs={{0,4},{4,8},{8,12},{12,16},{16,20},{20,24},{24,28},{1,5},{5,9},{9,... | collective-permute-start | bytes 24584 | tf_op jit(solution)/shard_map/ppermute | solution.py:25
  6.8 4.5 %collective-permute-start.5 = (f32[1,16,128]{2,1,0:T(8,128)S(1)}, f32[1,16,128]{2,1,0:T(8,128)S(1)}, u32[]{:S(2)}, u32[]{:S(2)}) collective-permute-start(f32[1,16,128]{2,1,0:T(8,128)S(1)} %get-tuple-element.79), channel_id=1, source_target_pairs={{4,0},{8,4},{12,8},{16,12},{20,16},{24,20},{28,24},{5,1},{9,5},{13... | collective-permute-start | bytes 24584 | tf_op jit(solution)/shard_map/ppermute | solution.py:27
  11.4 1.9 %collective-permute-start.4 = (f32[1,16,128]{2,1,0:T(8,128)S(1)}, f32[1,16,128]{2,1,0:T(8,128)S(1)}, u32[]{:S(2)}, u32[]{:S(2)}) collective-permute-start(f32[1,16,128]{2,1,0:T(8,128)S(1)} %get-tuple-element.80), channel_id=1, source_target_pairs={{0,4},{4,8},{8,12},{12,16},{16,20},{20,24},{24,28},{1,5},{5,9},{9,... | collective-permute-start | bytes 24584 | tf_op jit(solution)/shard_map/ppermute | solution.py:25
  14.1 4.5 %collective-permute-start.1 = (f32[3,1,16,128]{3,2,1,0:T(8,128)S(1)}, f32[3,1,16,128]{3,2,1,0:T(8,128)S(1)}, u32[]{:S(2)}, u32[]{:S(2)}) collective-permute-start(f32[3,1,16,128]{3,2,1,0:T(8,128)S(1)} %get-tuple-element.63), channel_id=1, source_target_pairs={{4,0},{8,4},{12,8},{16,12},{20,16},{24,20},{28,24},{5,1},{9,5},{13... | collective-permute-start | bytes 73736 | tf_op jit(solution)/shard_map/ppermute | solution.py:27
  21.9 1.9 %collective-permute-start = (f32[3,1,16,128]{3,2,1,0:T(8,128)S(1)}, f32[3,1,16,128]{3,2,1,0:T(8,128)S(1)}, u32[]{:S(2)}, u32[]{:S(2)}) collective-permute-start(f32[3,1,16,128]{3,2,1,0:T(8,128)S(1)} %get-tuple-element.64), channel_id=1, source_target_pairs={{0,4},{4,8},{8,12},{12,16},{16,20},{20,24},{24,28},{1,5},{5,9},{9,... | collective-permute-start | bytes 73736 | tf_op jit(solution)/shard_map/ppermute | solution.py:25
  25.8 3.5 %collective-permute-start.6 = (f32[10,1,128]{2,1,0:T(1,128)S(1)}, f32[10,1,128]{2,1,0:T(1,128)S(1)}, u32[]{:S(2)}, u32[]{:S(2)}) collective-permute-start(f32[10,1,128]{2,1,0:T(1,128)S(1)} %get-tuple-element.69), channel_id=1, source_target_pairs={{0,1},{1,2},{2,3},{4,5},{5,6},{6,7},{8,9},{9,10},{10,11},{12,13},{... | collective-permute-start | bytes 15368 | tf_op jit(solution)/shard_map/ppermute | solution.py:25
  29.4 2.4 %collective-permute-start.7 = (f32[10,1,128]{2,1,0:T(1,128)S(1)}, f32[10,1,128]{2,1,0:T(1,128)S(1)}, u32[]{:S(2)}, u32[]{:S(2)}) collective-permute-start(f32[10,1,128]{2,1,0:T(1,128)S(1)} %get-tuple-element.70), channel_id=1, source_target_pairs={{1,0},{2,1},{3,2},{5,4},{6,5},{7,6},{9,8},{10,9},{11,10},{13,12},{... | collective-permute-start | bytes 15368 | tf_op jit(solution)/shard_map/ppermute | solution.py:27
  31.8 3.5 %collective-permute-start.10 = (f32[10,1,128]{2,1,0:T(1,128)S(1)}, f32[10,1,128]{2,1,0:T(1,128)S(1)}, u32[]{:S(2)}, u32[]{:S(2)}) collective-permute-start(f32[10,1,128]{2,1,0:T(1,128)S(1)} %get-tuple-element.71), channel_id=1, source_target_pairs={{0,1},{1,2},{2,3},{4,5},{5,6},{6,7},{8,9},{9,10},{10,11},{12,13},{... | collective-permute-start | bytes 15368 | tf_op jit(solution)/shard_map/ppermute | solution.py:25
  35.3 2.3 %collective-permute-start.11 = (f32[10,1,128]{2,1,0:T(1,128)S(1)}, f32[10,1,128]{2,1,0:T(1,128)S(1)}, u32[]{:S(2)}, u32[]{:S(2)}) collective-permute-start(f32[10,1,128]{2,1,0:T(1,128)S(1)} %get-tuple-element.72), channel_id=1, source_target_pairs={{1,0},{2,1},{3,2},{5,4},{6,5},{7,6},{9,8},{10,9},{11,10},{13,12},{... | collective-permute-start | bytes 15368 | tf_op jit(solution)/shard_map/ppermute | solution.py:27
  37.8 3.5 %collective-permute-start.2 = (f32[3,10,1,128]{3,2,1,0:T(1,128)S(1)}, f32[3,10,1,128]{3,2,1,0:T(1,128)S(1)}, u32[]{:S(2)}, u32[]{:S(2)}) collective-permute-start(f32[3,10,1,128]{3,2,1,0:T(1,128)S(1)} %get-tuple-element.56), channel_id=1, source_target_pairs={{0,1},{1,2},{2,3},{4,5},{5,6},{6,7},{8,9},{9,10},{10,11},{12,13},{... | collective-permute-start | bytes 46088 | tf_op jit(solution)/shard_map/ppermute | solution.py:25
  41.3 2.3 %collective-permute-start.3 = (f32[3,10,1,128]{3,2,1,0:T(1,128)S(1)}, f32[3,10,1,128]{3,2,1,0:T(1,128)S(1)}, u32[]{:S(2)}, u32[]{:S(2)}) collective-permute-start(f32[3,10,1,128]{3,2,1,0:T(1,128)S(1)} %get-tuple-element.57), channel_id=1, source_target_pairs={{1,0},{2,1},{3,2},{5,4},{6,5},{7,6},{9,8},{10,9},{11,10},{13,12},{... | collective-permute-start | bytes 46088 | tf_op jit(solution)/shard_map/ppermute | solution.py:27
  43.7 3.2 %collective-permute-done.3 = f32[3,10,1,128]{3,2,1,0:T(1,128)S(1)} collective-permute-done((f32[3,10,1,128]{3,2,1,0:T(1,128)S(1)}, f32[3,10,1,128]{3,2,1,0:T(1,128)S(1)}, u32[]{:S(2)}, u32[]{:S(2)}) %collective-permute-start.3) | collective-permute-done | bytes 15392 | tf_op jit(solution)/shard_map/ppermute | solution.py:27
  47.8 2.1 %collective-permute-start.12 = (f32[3,1,16,128]{3,2,1,0:T(8,128)S(1)}, f32[3,1,16,128]{3,2,1,0:T(8,128)S(1)}, u32[]{:S(2)}, u32[]{:S(2)}) collective-permute-start(f32[3,1,16,128]{3,2,1,0:T(8,128)S(1)} %get-tuple-element.58), channel_id=1, source_target_pairs={{0,4},{4,8},{8,12},{12,16},{16,20},{20,24},{24,28},{1,5},{5,9},{9,... | collective-permute-start | bytes 73736 | tf_op jit(solution)/shard_map/ppermute | solution.py:25
  49.9 4.5 %collective-permute-start.13 = (f32[3,1,16,128]{3,2,1,0:T(8,128)S(1)}, f32[3,1,16,128]{3,2,1,0:T(8,128)S(1)}, u32[]{:S(2)}, u32[]{:S(2)}) collective-permute-start(f32[3,1,16,128]{3,2,1,0:T(8,128)S(1)} %get-tuple-element.59), channel_id=1, source_target_pairs={{4,0},{8,4},{12,8},{16,12},{20,16},{24,20},{28,24},{5,1},{9,5},{13... | collective-permute-start | bytes 73736 | tf_op jit(solution)/shard_map/ppermute | solution.py:27
  56.0 3.5 %collective-permute-start.14 = (f32[3,10,1,128]{3,2,1,0:T(1,128)S(1)}, f32[3,10,1,128]{3,2,1,0:T(1,128)S(1)}, u32[]{:S(2)}, u32[]{:S(2)}) collective-permute-start(f32[3,10,1,128]{3,2,1,0:T(1,128)S(1)} %get-tuple-element.48), channel_id=1, source_target_pairs={{0,1},{1,2},{2,3},{4,5},{5,6},{6,7},{8,9},{9,10},{10,11},{12,13},{... | collective-permute-start | bytes 46088 | tf_op jit(solution)/shard_map/ppermute | solution.py:25
  59.5 2.4 %collective-permute-start.15 = (f32[3,10,1,128]{3,2,1,0:T(1,128)S(1)}, f32[3,10,1,128]{3,2,1,0:T(1,128)S(1)}, u32[]{:S(2)}, u32[]{:S(2)}) collective-permute-start(f32[3,10,1,128]{3,2,1,0:T(1,128)S(1)} %get-tuple-element.49), channel_id=1, source_target_pairs={{1,0},{2,1},{3,2},{5,4},{6,5},{7,6},{9,8},{10,9},{11,10},{13,12},{... | collective-permute-start | bytes 46088 | tf_op jit(solution)/shard_map/ppermute | solution.py:27
  64.3 4.5 %collective-permute-start.18 = (f32[1,16,128]{2,1,0:T(8,128)S(1)}, f32[1,16,128]{2,1,0:T(8,128)S(1)}, u32[]{:S(2)}, u32[]{:S(2)}) collective-permute-start(f32[1,16,128]{2,1,0:T(8,128)S(1)} %get-tuple-element.78), channel_id=1, source_target_pairs={{4,0},{8,4},{12,8},{16,12},{20,16},{24,20},{28,24},{5,1},{9,5},{13... | collective-permute-start | bytes 24584 | tf_op jit(solution)/shard_map/ppermute | solution.py:27
  70.9 4.5 %collective-permute-start.22 = (f32[1,16,128]{2,1,0:T(8,128)S(1)}, f32[1,16,128]{2,1,0:T(8,128)S(1)}, u32[]{:S(2)}, u32[]{:S(2)}) collective-permute-start(f32[1,16,128]{2,1,0:T(8,128)S(1)} %get-tuple-element.76), channel_id=1, source_target_pairs={{4,0},{8,4},{12,8},{16,12},{20,16},{24,20},{28,24},{5,1},{9,5},{13... | collective-permute-start | bytes 24584 | tf_op jit(solution)/shard_map/ppermute | solution.py:27
  77.4 3.5 %collective-permute-start.19 = (f32[10,1,128]{2,1,0:T(1,128)S(1)}, f32[10,1,128]{2,1,0:T(1,128)S(1)}, u32[]{:S(2)}, u32[]{:S(2)}) collective-permute-start(f32[10,1,128]{2,1,0:T(1,128)S(1)} %get-tuple-element.67), channel_id=1, source_target_pairs={{0,1},{1,2},{2,3},{4,5},{5,6},{6,7},{8,9},{9,10},{10,11},{12,13},{... | collective-permute-start | bytes 15368 | tf_op jit(solution)/shard_map/ppermute | solution.py:25
  80.9 2.4 %collective-permute-start.20 = (f32[10,1,128]{2,1,0:T(1,128)S(1)}, f32[10,1,128]{2,1,0:T(1,128)S(1)}, u32[]{:S(2)}, u32[]{:S(2)}) collective-permute-start(f32[10,1,128]{2,1,0:T(1,128)S(1)} %get-tuple-element.68), channel_id=1, source_target_pairs={{1,0},{2,1},{3,2},{5,4},{6,5},{7,6},{9,8},{10,9},{11,10},{13,12},{... | collective-permute-start | bytes 15368 | tf_op jit(solution)/shard_map/ppermute | solution.py:27
  83.3 3.5 %collective-permute-start.23 = (f32[10,1,128]{2,1,0:T(1,128)S(1)}, f32[10,1,128]{2,1,0:T(1,128)S(1)}, u32[]{:S(2)}, u32[]{:S(2)}) collective-permute-start(f32[10,1,128]{2,1,0:T(1,128)S(1)} %get-tuple-element.65), channel_id=1, source_target_pairs={{0,1},{1,2},{2,3},{4,5},{5,6},{6,7},{8,9},{9,10},{10,11},{12,13},{... | collective-permute-start | bytes 15368 | tf_op jit(solution)/shard_map/ppermute | solution.py:25
  86.8 2.4 %collective-permute-start.24 = (f32[10,1,128]{2,1,0:T(1,128)S(1)}, f32[10,1,128]{2,1,0:T(1,128)S(1)}, u32[]{:S(2)}, u32[]{:S(2)}) collective-permute-start(f32[10,1,128]{2,1,0:T(1,128)S(1)} %get-tuple-element.66), channel_id=1, source_target_pairs={{1,0},{2,1},{3,2},{5,4},{6,5},{7,6},{9,8},{10,9},{11,10},{13,12},{... | collective-permute-start | bytes 15368 | tf_op jit(solution)/shard_map/ppermute | solution.py:27
  89.2 3.1 %collective-permute-done.24 = f32[10,1,128]{2,1,0:T(1,128)S(1)} collective-permute-done((f32[10,1,128]{2,1,0:T(1,128)S(1)}, f32[10,1,128]{2,1,0:T(1,128)S(1)}, u32[]{:S(2)}, u32[]{:S(2)}) %collective-permute-start.24) | collective-permute-done | bytes 5152 | tf_op jit(solution)/shard_map/ppermute | solution.py:27
  (101 shorter events, 20.3 us)
Async XLA Ops:
  1.4 27.9 %collective-permute-start.9 = (f32[1,16,128]{2,1,0:T(8,128)S(1)}, f32[1,16,128]{2,1,0:T(8,128)S(1)}, u32[]{:S(2)}, u32[]{:S(2)}) collective-permute-start(f32[1,16,128]{2,1,0:T(8,128)S(1)} %get-tuple-element.81), channel_id=1, source_target_pairs={{4,0},{8,4},{12,8},{16,12},{20,16},{24,20},{28,24},{5,1},{9,5},{13... | collective-permute-start | bytes 24584 | tf_op jit(solution)/shard_map/ppermute | solution.py:27
  4.2 21.6 %collective-permute-start.8 = (f32[1,16,128]{2,1,0:T(8,128)S(1)}, f32[1,16,128]{2,1,0:T(8,128)S(1)}, u32[]{:S(2)}, u32[]{:S(2)}) collective-permute-start(f32[1,16,128]{2,1,0:T(8,128)S(1)} %get-tuple-element.82), channel_id=1, source_target_pairs={{0,4},{4,8},{8,12},{12,16},{16,20},{20,24},{24,28},{1,5},{5,9},{9,... | collective-permute-start | bytes 24584 | tf_op jit(solution)/shard_map/ppermute | solution.py:25
  6.8 17.0 %collective-permute-start.5 = (f32[1,16,128]{2,1,0:T(8,128)S(1)}, f32[1,16,128]{2,1,0:T(8,128)S(1)}, u32[]{:S(2)}, u32[]{:S(2)}) collective-permute-start(f32[1,16,128]{2,1,0:T(8,128)S(1)} %get-tuple-element.79), channel_id=1, source_target_pairs={{4,0},{8,4},{12,8},{16,12},{20,16},{24,20},{28,24},{5,1},{9,5},{13... | collective-permute-start | bytes 24584 | tf_op jit(solution)/shard_map/ppermute | solution.py:27
  11.4 10.5 %collective-permute-start.4 = (f32[1,16,128]{2,1,0:T(8,128)S(1)}, f32[1,16,128]{2,1,0:T(8,128)S(1)}, u32[]{:S(2)}, u32[]{:S(2)}) collective-permute-start(f32[1,16,128]{2,1,0:T(8,128)S(1)} %get-tuple-element.80), channel_id=1, source_target_pairs={{0,4},{4,8},{8,12},{12,16},{16,20},{20,24},{24,28},{1,5},{5,9},{9,... | collective-permute-start | bytes 24584 | tf_op jit(solution)/shard_map/ppermute | solution.py:25
  14.1 23.6 %collective-permute-start.1 = (f32[3,1,16,128]{3,2,1,0:T(8,128)S(1)}, f32[3,1,16,128]{3,2,1,0:T(8,128)S(1)}, u32[]{:S(2)}, u32[]{:S(2)}) collective-permute-start(f32[3,1,16,128]{3,2,1,0:T(8,128)S(1)} %get-tuple-element.63), channel_id=1, source_target_pairs={{4,0},{8,4},{12,8},{16,12},{20,16},{24,20},{28,24},{5,1},{9,5},{13... | collective-permute-start | bytes 73736 | tf_op jit(solution)/shard_map/ppermute | solution.py:27
  21.9 15.8 %collective-permute-start = (f32[3,1,16,128]{3,2,1,0:T(8,128)S(1)}, f32[3,1,16,128]{3,2,1,0:T(8,128)S(1)}, u32[]{:S(2)}, u32[]{:S(2)}) collective-permute-start(f32[3,1,16,128]{3,2,1,0:T(8,128)S(1)} %get-tuple-element.64), channel_id=1, source_target_pairs={{0,4},{4,8},{8,12},{12,16},{16,20},{20,24},{24,28},{1,5},{5,9},{9,... | collective-permute-start | bytes 73736 | tf_op jit(solution)/shard_map/ppermute | solution.py:25
  23.9 38.0 %collective-permute-start.16 = (f32[17,16,128]{2,1,0:T(8,128)S(1)}, f32[17,16,128]{2,1,0:T(8,128)S(1)}, u32[]{:S(2)}, u32[]{:S(2)}) collective-permute-start(f32[17,16,128]{2,1,0:T(8,128)S(1)} %pad_maximum_fusion.3), channel_id=1, source_target_pairs={{0,4},{4,8},{8,12},{12,16},{16,20},{20,24},{24,28},{1,5},{5,9},{9,... | collective-permute-start | bytes 417800 | tf_op jit(solution)/shard_map/ppermute | solution.py:37
  25.8 5.9 %collective-permute-start.6 = (f32[10,1,128]{2,1,0:T(1,128)S(1)}, f32[10,1,128]{2,1,0:T(1,128)S(1)}, u32[]{:S(2)}, u32[]{:S(2)}) collective-permute-start(f32[10,1,128]{2,1,0:T(1,128)S(1)} %get-tuple-element.69), channel_id=1, source_target_pairs={{0,1},{1,2},{2,3},{4,5},{5,6},{6,7},{8,9},{9,10},{10,11},{12,13},{... | collective-permute-start | bytes 15368 | tf_op jit(solution)/shard_map/ppermute | solution.py:25
  29.4 5.9 %collective-permute-start.7 = (f32[10,1,128]{2,1,0:T(1,128)S(1)}, f32[10,1,128]{2,1,0:T(1,128)S(1)}, u32[]{:S(2)}, u32[]{:S(2)}) collective-permute-start(f32[10,1,128]{2,1,0:T(1,128)S(1)} %get-tuple-element.70), channel_id=1, source_target_pairs={{1,0},{2,1},{3,2},{5,4},{6,5},{7,6},{9,8},{10,9},{11,10},{13,12},{... | collective-permute-start | bytes 15368 | tf_op jit(solution)/shard_map/ppermute | solution.py:27
  31.8 11.9 %collective-permute-start.10 = (f32[10,1,128]{2,1,0:T(1,128)S(1)}, f32[10,1,128]{2,1,0:T(1,128)S(1)}, u32[]{:S(2)}, u32[]{:S(2)}) collective-permute-start(f32[10,1,128]{2,1,0:T(1,128)S(1)} %get-tuple-element.71), channel_id=1, source_target_pairs={{0,1},{1,2},{2,3},{4,5},{5,6},{6,7},{8,9},{9,10},{10,11},{12,13},{... | collective-permute-start | bytes 15368 | tf_op jit(solution)/shard_map/ppermute | solution.py:25
  35.3 8.4 %collective-permute-start.11 = (f32[10,1,128]{2,1,0:T(1,128)S(1)}, f32[10,1,128]{2,1,0:T(1,128)S(1)}, u32[]{:S(2)}, u32[]{:S(2)}) collective-permute-start(f32[10,1,128]{2,1,0:T(1,128)S(1)} %get-tuple-element.72), channel_id=1, source_target_pairs={{1,0},{2,1},{3,2},{5,4},{6,5},{7,6},{9,8},{10,9},{11,10},{13,12},{... | collective-permute-start | bytes 15368 | tf_op jit(solution)/shard_map/ppermute | solution.py:27
  37.8 5.9 %collective-permute-start.2 = (f32[3,10,1,128]{3,2,1,0:T(1,128)S(1)}, f32[3,10,1,128]{3,2,1,0:T(1,128)S(1)}, u32[]{:S(2)}, u32[]{:S(2)}) collective-permute-start(f32[3,10,1,128]{3,2,1,0:T(1,128)S(1)} %get-tuple-element.56), channel_id=1, source_target_pairs={{0,1},{1,2},{2,3},{4,5},{5,6},{6,7},{8,9},{9,10},{10,11},{12,13},{... | collective-permute-start | bytes 46088 | tf_op jit(solution)/shard_map/ppermute | solution.py:25
  47.8 6.8 %collective-permute-start.12 = (f32[3,1,16,128]{3,2,1,0:T(8,128)S(1)}, f32[3,1,16,128]{3,2,1,0:T(8,128)S(1)}, u32[]{:S(2)}, u32[]{:S(2)}) collective-permute-start(f32[3,1,16,128]{3,2,1,0:T(8,128)S(1)} %get-tuple-element.58), channel_id=1, source_target_pairs={{0,4},{4,8},{8,12},{12,16},{16,20},{20,24},{24,28},{1,5},{5,9},{9,... | collective-permute-start | bytes 73736 | tf_op jit(solution)/shard_map/ppermute | solution.py:25
  49.9 6.0 %collective-permute-start.13 = (f32[3,1,16,128]{3,2,1,0:T(8,128)S(1)}, f32[3,1,16,128]{3,2,1,0:T(8,128)S(1)}, u32[]{:S(2)}, u32[]{:S(2)}) collective-permute-start(f32[3,1,16,128]{3,2,1,0:T(8,128)S(1)} %get-tuple-element.59), channel_id=1, source_target_pairs={{4,0},{8,4},{12,8},{16,12},{20,16},{24,20},{28,24},{5,1},{9,5},{13... | collective-permute-start | bytes 73736 | tf_op jit(solution)/shard_map/ppermute | solution.py:27
  56.0 36.4 %collective-permute-start.14 = (f32[3,10,1,128]{3,2,1,0:T(1,128)S(1)}, f32[3,10,1,128]{3,2,1,0:T(1,128)S(1)}, u32[]{:S(2)}, u32[]{:S(2)}) collective-permute-start(f32[3,10,1,128]{3,2,1,0:T(1,128)S(1)} %get-tuple-element.48), channel_id=1, source_target_pairs={{0,1},{1,2},{2,3},{4,5},{5,6},{6,7},{8,9},{9,10},{10,11},{12,13},{... | collective-permute-start | bytes 46088 | tf_op jit(solution)/shard_map/ppermute | solution.py:25
  59.5 32.9 %collective-permute-start.15 = (f32[3,10,1,128]{3,2,1,0:T(1,128)S(1)}, f32[3,10,1,128]{3,2,1,0:T(1,128)S(1)}, u32[]{:S(2)}, u32[]{:S(2)}) collective-permute-start(f32[3,10,1,128]{3,2,1,0:T(1,128)S(1)} %get-tuple-element.49), channel_id=1, source_target_pairs={{1,0},{2,1},{3,2},{5,4},{6,5},{7,6},{9,8},{10,9},{11,10},{13,12},{... | collective-permute-start | bytes 46088 | tf_op jit(solution)/shard_map/ppermute | solution.py:27
  62.3 8.5 %collective-permute-start.17 = (f32[1,16,128]{2,1,0:T(8,128)S(1)}, f32[1,16,128]{2,1,0:T(8,128)S(1)}, u32[]{:S(2)}, u32[]{:S(2)}) collective-permute-start(f32[1,16,128]{2,1,0:T(8,128)S(1)} %get-tuple-element.77), channel_id=1, source_target_pairs={{0,4},{4,8},{8,12},{12,16},{16,20},{20,24},{24,28},{1,5},{5,9},{9,... | collective-permute-start | bytes 24584 | tf_op jit(solution)/shard_map/ppermute | solution.py:25
  64.3 11.2 %collective-permute-start.18 = (f32[1,16,128]{2,1,0:T(8,128)S(1)}, f32[1,16,128]{2,1,0:T(8,128)S(1)}, u32[]{:S(2)}, u32[]{:S(2)}) collective-permute-start(f32[1,16,128]{2,1,0:T(8,128)S(1)} %get-tuple-element.78), channel_id=1, source_target_pairs={{4,0},{8,4},{12,8},{16,12},{20,16},{24,20},{28,24},{5,1},{9,5},{13... | collective-permute-start | bytes 24584 | tf_op jit(solution)/shard_map/ppermute | solution.py:27
  68.9 8.4 %collective-permute-start.21 = (f32[1,16,128]{2,1,0:T(8,128)S(1)}, f32[1,16,128]{2,1,0:T(8,128)S(1)}, u32[]{:S(2)}, u32[]{:S(2)}) collective-permute-start(f32[1,16,128]{2,1,0:T(8,128)S(1)} %get-tuple-element.75), channel_id=1, source_target_pairs={{0,4},{4,8},{8,12},{12,16},{16,20},{20,24},{24,28},{1,5},{5,9},{9,... | collective-permute-start | bytes 24584 | tf_op jit(solution)/shard_map/ppermute | solution.py:25
  70.9 10.0 %collective-permute-start.22 = (f32[1,16,128]{2,1,0:T(8,128)S(1)}, f32[1,16,128]{2,1,0:T(8,128)S(1)}, u32[]{:S(2)}, u32[]{:S(2)}) collective-permute-start(f32[1,16,128]{2,1,0:T(8,128)S(1)} %get-tuple-element.76), channel_id=1, source_target_pairs={{4,0},{8,4},{12,8},{16,12},{20,16},{24,20},{28,24},{5,1},{9,5},{13... | collective-permute-start | bytes 24584 | tf_op jit(solution)/shard_map/ppermute | solution.py:27
  75.4 18.5 %collective-permute-start.25 = (f32[17,16,128]{2,1,0:T(8,128)S(1)}, f32[17,16,128]{2,1,0:T(8,128)S(1)}, u32[]{:S(2)}, u32[]{:S(2)}) collective-permute-start(f32[17,16,128]{2,1,0:T(8,128)S(1)} %pad_maximum_fusion.4), channel_id=1, source_target_pairs={{0,4},{4,8},{8,12},{12,16},{16,20},{20,24},{24,28},{1,5},{5,9},{9,... | collective-permute-start | bytes 417800 | tf_op jit(solution)/shard_map/ppermute | solution.py:37
  77.4 5.9 %collective-permute-start.19 = (f32[10,1,128]{2,1,0:T(1,128)S(1)}, f32[10,1,128]{2,1,0:T(1,128)S(1)}, u32[]{:S(2)}, u32[]{:S(2)}) collective-permute-start(f32[10,1,128]{2,1,0:T(1,128)S(1)} %get-tuple-element.67), channel_id=1, source_target_pairs={{0,1},{1,2},{2,3},{4,5},{5,6},{6,7},{8,9},{9,10},{10,11},{12,13},{... | collective-permute-start | bytes 15368 | tf_op jit(solution)/shard_map/ppermute | solution.py:25
  80.9 5.9 %collective-permute-start.20 = (f32[10,1,128]{2,1,0:T(1,128)S(1)}, f32[10,1,128]{2,1,0:T(1,128)S(1)}, u32[]{:S(2)}, u32[]{:S(2)}) collective-permute-start(f32[10,1,128]{2,1,0:T(1,128)S(1)} %get-tuple-element.68), channel_id=1, source_target_pairs={{1,0},{2,1},{3,2},{5,4},{6,5},{7,6},{9,8},{10,9},{11,10},{13,12},{... | collective-permute-start | bytes 15368 | tf_op jit(solution)/shard_map/ppermute | solution.py:27
  83.3 5.9 %collective-permute-start.23 = (f32[10,1,128]{2,1,0:T(1,128)S(1)}, f32[10,1,128]{2,1,0:T(1,128)S(1)}, u32[]{:S(2)}, u32[]{:S(2)}) collective-permute-start(f32[10,1,128]{2,1,0:T(1,128)S(1)} %get-tuple-element.65), channel_id=1, source_target_pairs={{0,1},{1,2},{2,3},{4,5},{5,6},{6,7},{8,9},{9,10},{10,11},{12,13},{... | collective-permute-start | bytes 15368 | tf_op jit(solution)/shard_map/ppermute | solution.py:25
  (9 other events, 128.8 us)
where the time goes:
time: 97.6 us; the launch traced here: 96.3 us
  starting transfers between devices  76 us (78%)
  waiting for transfers between devices  7.67 us (8%)
  other arithmetic  6.55 us (7%)
  local copies, waits for them, and re-layouts  4.69 us (5%)
  between operations  1.45 us (1%)
    ppermute x12, starting transfers between devices, extended(): lax.ppermute(head, axis, [((i + 1) % count, i) for i in range(ends)])  39.6 us
    ppermute x12, starting transfers between devices, extended(): lax.ppermute(tail, axis, [(i, (i + 1) % count) for i in range(ends)])  32.6 us
    ppermute x12, waiting for transfers between devices, extended(): lax.ppermute(head, axis, [((i + 1) % count, i) for i in range(ends)])  7.63 us
    ppermute x2, starting transfers between devices, passed_along(): return lax.ppermute(block, axis, route)  3.84 us
    slice x3, local copies, waits for them, and re-layouts, extended(): head = lax.slice_in_dim(cells, 0, width, axis=dim)  2.24 us
  transfers between devices with their start and end apart: 26, of which 3 were waited for; matrix products, arithmetic and copies ran while one was open for 8% of the time, Pallas kernels for 0%

commit v1 on v0

v1 whole, which is shorter than its diff:
```python
import functools

import jax
import jax.numpy as jnp
from jax import lax
from jax.experimental import pallas as pl
from jax.experimental.pallas import tpu as pltpu
from jax.sharding import PartitionSpec as P

visc_base = 0.2
time_step = 0.1
buoyancy = 0.5
drag_rate = 0.3
vent_speed = 1.0
inject_rate = 0.5
evap_rate = 0.4
latent_heat = 0.5
scavenge = 0.3

MESH = pl.DeviceIdType.MESH
FIELDS = 5
LOAD, TALLY, SPRAY = 5, 6, 7
ALL = 8


def shifted(c, lane):
    rows, depth = c.shape
    below = pltpu.roll(c, 1, 0)
    above = pltpu.roll(c, rows - 1, 0)
    down = jnp.where(lane == 0, 0.0, pltpu.roll(c, 1, 1))
    up = jnp.where(lane == depth - 1, 0.0, pltpu.roll(c, depth - 1, 1))
    return below, above, down, up


def transported(q, behind, ahead, th, th_behind, th_ahead, lane, keep):
    cut = lambda a: a[:keep]
    around_th = [cut(a) for a in shifted(th, lane)]
    th0 = cut(th)
    half = 0.5 * time_step
    base = 2.0 * visc_base * half
    slope = 0.5 * visc_base * half
    mine = base + slope * th0
    wind = [half * cut(q[d]) for d in range(3)]
    a = [mine + slope * t for t in [cut(th_behind), cut(th_ahead)] + around_th]
    weights = [
        a[0] + wind[0], a[1] - wind[0],
        a[2] + wind[1], a[3] - wind[1],
        a[4] + wind[2], a[5] - wind[2],
    ]
    own = 1.0 - ((a[0] + a[1]) + (a[2] + a[3]) + (a[4] + a[5]))
    fresh = []
    for f in range(FIELDS):
        near = [cut(behind[f]), cut(ahead[f])] + [cut(s) for s in shifted(q[f], lane)]
        terms = [w * n for w, n in zip(weights, near)]
        fresh.append(
            (own * cut(q[f]) + terms[0])
            + (terms[1] + terms[2])
            + (terms[3] + terms[4])
            + terms[5]
        )
    fresh[0] = fresh[0] + time_step * drag_rate * (vent_speed - cut(q[0]))
    fresh[2] = fresh[2] + time_step * buoyancy * cut(q[3])
    return fresh


def droplet(heat, soot, sprayed):
    kept = (1.0 - 0.5 * evap_rate) - 0.5 * evap_rate * jnp.tanh(0.5 * heat)
    heat = heat - latent_heat * (1.0 - kept) * sprayed
    soot = soot / (1.0 + scavenge * sprayed)
    return heat, soot, kept


def exchange_kernel(
    tun_size, sec_size,
    wind_hbm, heat_hbm, soot_hbm, mass_hbm, count_hbm, label_hbm, onset,
    state, coef, mass_in,
    ext, first, kept_first, spray_next, mass, count, label,
    pack_low, pack_high, from_low, from_high,
    local_sem, send_sem, recv_sem,
):
    X, Y, Z = heat_hbm.shape
    slots = mass_hbm.shape[0]
    t, s = lax.axis_index("tun"), lax.axis_index("sec")
    has = {-1: t > 0, 1: t < tun_size - 1}
    has_sec = {-1: s > 0, 1: s < sec_size - 1}

    def exists(dt, ds):
        if dt and ds:
            return jnp.logical_and(has[dt], has_sec[ds])
        return has[dt] if dt else has_sec[ds]

    around = [(a, b) for a in (-1, 0, 1) for b in (-1, 0, 1) if a or b]

    def load(i, src, dst):
        return pltpu.make_async_copy(src, dst, local_sem.at[i])

    loads = [
        load(0, count_hbm, count),
        load(1, label_hbm, label),
        load(2, mass_hbm, mass),
        load(3, wind_hbm, ext.at[0:3, 2:X + 2, 0:Y]),
        load(4, heat_hbm, ext.at[3, 2:X + 2, 0:Y]),
        load(5, soot_hbm, ext.at[4, 2:X + 2, 0:Y]),
    ]
    for c in loads:
        c.start()

    barrier = pltpu.get_barrier_semaphore()
    for a, b in around:
        @pl.when(exists(a, b))
        def _(a=a, b=b):
            pl.semaphore_signal(
                barrier, inc=1, device_id={"tun": t + a, "sec": s + b}, device_id_type=MESH
            )
    wide = has[-1].astype(jnp.int32) + has[1].astype(jnp.int32)
    deep = has_sec[-1].astype(jnp.int32) + has_sec[1].astype(jnp.int32)
    pl.semaphore_wait(barrier, (1 + wide) * (1 + deep) - 1)

    def send(i, a, b, src, dst):
        return (a, b, pltpu.make_async_remote_copy(
            src_ref=src, dst_ref=dst, send_sem=send_sem.at[i], recv_sem=recv_sem.at[i],
            device_id={"tun": t + a, "sec": s + b}, device_id_type=MESH,
        ))

    def start(group):
        for a, b, copy in group:
            @pl.when(exists(a, b))
            def _(copy=copy):
                copy.start()

    def wait_recv(group):
        for a, b, copy in group:
            @pl.when(exists(-a, -b))
            def _(copy=copy):
                copy.wait_recv()

    fields = [
        send(0, 1, 0, wind_hbm.at[:, X - 2:X], ext.at[0:3, 0:2, 0:Y]),
        send(1, 1, 0, heat_hbm.at[X - 2:X], ext.at[3, 0:2, 0:Y]),
        send(2, 1, 0, soot_hbm.at[X - 2:X], ext.at[4, 0:2, 0:Y]),
        send(3, -1, 0, wind_hbm.at[:, 0:2], ext.at[0:3, X + 2:X + 4, 0:Y]),
        send(4, -1, 0, heat_hbm.at[0:2], ext.at[3, X + 2:X + 4, 0:Y]),
        send(5, -1, 0, soot_hbm.at[0:2], ext.at[4, X + 2:X + 4, 0:Y]),
    ]
    start(fields)

    for c in loads[:3]:
        c.wait()

    def sums(x, _):
        n = count[x]
        terms = [jnp.where(n > k, mass[k, x], 0.0) for k in range(slots)]
        while len(terms) > 1:
            terms = [terms[i] + terms[i + 1] for i in range(0, len(terms) - 1, 2)] + (
                [terms[-1]] if len(terms) % 2 else [])
        zone = label[x]
        onset_here = jnp.full((Y, Z), 1 << 20, jnp.int32)
        for z in range(onset.shape[0]):
            onset_here = jnp.where(zone == z + 1, onset[z], onset_here)
        ext[LOAD, x + 2, 0:Y] = terms[0]
        ext[TALLY, x + 2, 0:Y] = n.astype(jnp.float32)
        ext[SPRAY, x + 2, 0:Y] = jnp.where(onset_here <= 0, inject_rate, 0.0)
        spray_next[x] = jnp.where(onset_here <= 1, inject_rate, 0.0)
        return 0

    lax.fori_loop(0, X, sums, 0)
    drops = [
        send(6, 1, 0, ext.at[LOAD:ALL, X:X + 2, 0:Y], ext.at[LOAD:ALL, 0:2, 0:Y]),
        send(7, -1, 0, ext.at[SPRAY, 2:4, 0:Y], ext.at[SPRAY, X + 2:X + 4, 0:Y]),
    ]
    start(drops)
    for c in loads[3:]:
        c.wait()

    row = lax.broadcasted_iota(jnp.int32, (8, Z), 0)

    def packing(x, _):
        for g in range(2):
            low = high = None
            for j in range(4):
                f = 4 * g + j
                tile_low = ext[f, x + 2, 0:8]
                tile_high = ext[f, x + 2, Y - 8:Y]
                if j == 0:
                    low, high = tile_low, tile_high
                else:
                    here = jnp.logical_and(row >= 2 * j, row < 2 * j + 2)
                    low = jnp.where(here, pltpu.roll(tile_low, 2 * j, 0), low)
                    place = (2 * j + 6) % 8
                    there = jnp.logical_and(row >= place, row < place + 2)
                    high = jnp.where(there, pltpu.roll(tile_high, 2 * j, 0), high)
            pack_low[x, g] = low
            pack_high[x, g] = high
        return 0

    lax.fori_loop(0, X, packing, 0)
    across = [
        send(8, 0, -1, pack_low, from_high.at[1:X + 1]),
        send(9, 0, 1, pack_high, from_low.at[1:X + 1]),
        send(10, -1, -1, pack_low.at[0], from_high.at[X + 1]),
        send(11, 1, -1, pack_low.at[X - 1], from_high.at[0]),
        send(12, -1, 1, pack_high.at[0], from_low.at[X + 1]),
        send(13, 1, 1, pack_high.at[X - 1], from_low.at[0]),
    ]
    start(across)
    masses = [send(14, 1, 0, mass_hbm.at[:, X - 2:X], mass_in)]
    start(masses)

    @pl.when(jnp.logical_not(has[-1]))
    def _():
        ext[:, 0:2] = jnp.zeros((ALL, 2) + ext.shape[2:], jnp.float32)
        from_low[0] = jnp.zeros(from_low.shape[1:], jnp.float32)
        from_high[0] = jnp.zeros(from_low.shape[1:], jnp.float32)
        mass_in[...] = jnp.zeros(mass_in.shape, jnp.float32)

    @pl.when(jnp.logical_not(has[1]))
    def _():
        ext[:, X + 2:X + 4] = jnp.zeros((ALL, 2) + ext.shape[2:], jnp.float32)
        from_low[X + 1] = jnp.zeros(from_low.shape[1:], jnp.float32)
        from_high[X + 1] = jnp.zeros(from_low.shape[1:], jnp.float32)

    @pl.when(jnp.logical_not(has_sec[-1]))
    def _():
        from_low[...] = jnp.zeros(from_low.shape, jnp.float32)

    @pl.when(jnp.logical_not(has_sec[1]))
    def _():
        from_high[...] = jnp.zeros(from_high.shape, jnp.float32)

    wait_recv(fields + drops + across)

    def unpacking(p, _):
        for g in range(2):
            high, low = from_high[p], from_low[p]
            for j in range(4):
                here = jnp.logical_and(row >= 2 * j, row < 2 * j + 2)
                tile = jnp.where(here, high[g], low[g])
                if j:
                    tile = pltpu.roll(tile, 8 - 2 * j, 0)
                ext[4 * g + j, p + 1, Y:Y + 8] = tile
        return 0

    lax.fori_loop(0, X + 2, unpacking, 0)

    lane = lax.broadcasted_iota(jnp.int32, (Y + 8, Z), 1)

    def substep_first(p, carry):
        th_behind, th = carry
        th_ahead = jnp.tanh(ext[3, p + 1])
        q = [ext[f, p] for f in range(FIELDS)]
        behind = [ext[f, p - 1] for f in range(FIELDS)]
        ahead = [ext[f, p + 1] for f in range(FIELDS)]
        fresh = transported(q, behind, ahead, th, th_behind, th_ahead, lane, Y + 8)
        sprayed = ext[LOAD, p - 1] + ext[SPRAY, p] * ext[TALLY, p - 1]
        fresh[3], fresh[4], kept = droplet(fresh[3], fresh[4], sprayed)
        for f in range(FIELDS):
            first[f, p - 1] = fresh[f]
        first[LOAD, p - 1] = kept * sprayed
        kept_first[p - 1] = kept[:Y]
        return th, th_ahead

    lax.fori_loop(1, X + 3, substep_first, (jnp.tanh(ext[3, 0]), jnp.tanh(ext[3, 1])))

    @pl.when(jnp.logical_not(has[-1]))
    def _():
        first[:, 0] = jnp.zeros((first.shape[0],) + first.shape[2:], jnp.float32)

    @pl.when(jnp.logical_not(has[1]))
    def _():
        first[:, X + 1] = jnp.zeros((first.shape[0],) + first.shape[2:], jnp.float32)

    @pl.when(jnp.logical_not(has_sec[-1]))
    def _():
        first[:, :, Y + 7:Y + 8] = jnp.zeros(first.shape[:2] + (1, Z), jnp.float32)

    @pl.when(jnp.logical_not(has_sec[1]))
    def _():
        first[:, :, Y:Y + 1] = jnp.zeros(first.shape[:2] + (1, Z), jnp.float32)

    def substep_second(p, carry):
        th_behind, th = carry
        x = p - 1
        th_ahead = jnp.tanh(first[3, p + 1])
        q = [first[f, p] for f in range(FIELDS)]
        behind = [first[f, p - 1] for f in range(FIELDS)]
        ahead = [first[f, p + 1] for f in range(FIELDS)]
        fresh = transported(q, behind, ahead, th, th_behind, th_ahead, lane, Y)
        tally = ext[TALLY, x, 0:Y]
        spray = spray_next[x]
        sprayed = first[LOAD, p - 1, 0:Y] + spray * tally
        fresh[3], fresh[4], kept = droplet(fresh[3], fresh[4], sprayed)
        for f in range(FIELDS):
            state[f, x] = fresh[f]
        before = kept_first[p - 1]
        coef[0, x] = before * kept
        coef[1, x] = (ext[SPRAY, x + 1, 0:Y] * before + spray) * kept
        coef[2, x] = tally
        return th, th_ahead

    lax.fori_loop(1, X + 1, substep_second, (jnp.tanh(first[3, 0]), jnp.tanh(first[3, 1])))

    wait_recv(masses)
    for a, b, copy in fields + drops + across + masses:
        @pl.when(exists(a, b))
        def _(copy=copy):
            copy.wait_send()


def droplet_kernel(
    chunk, mass_hbm, state, coef, mass_in,
    wind_out, heat_out, soot_out, mass_out, count_out,
    mass, fresh, tally, in_sem, out_sem, state_sem,
):
    slots, X = mass_hbm.shape[:2]
    parts = slots // chunk
    loads = [
        pltpu.make_async_copy(
            mass_hbm.at[pl.ds(i * chunk, chunk), 0:X - 2], mass.at[pl.ds(i * chunk, chunk)],
            in_sem.at[i],
        )
        for i in range(parts)
    ]
    for c in loads:
        c.start()
    moves = [
        pltpu.make_async_copy(state.at[0:3], wind_out, state_sem.at[0]),
        pltpu.make_async_copy(state.at[3], heat_out, state_sem.at[1]),
        pltpu.make_async_copy(state.at[4], soot_out, state_sem.at[2]),
        pltpu.make_async_copy(tally, count_out, state_sem.at[3]),
    ]
    for c in moves[:3]:
        c.start()
    tally[...] = coef[2].astype(jnp.int32)
    moves[3].start()
    stores = []
    for i in range(parts):
        if i == 0:
            def edge(x, _):
                keep, add, n = coef[0, x], coef[1, x], coef[2, x]
                for k in range(slots):
                    m = mass_in[k, x]
                    fresh[k, x] = jnp.where(n > k, keep * m + add, m)
                return 0

            lax.fori_loop(0, 2, edge, 0)
        loads[i].wait()

        def inner(x, _, i=i):
            keep, add, n = coef[0, x], coef[1, x], coef[2, x]
            for k in range(i * chunk, (i + 1) * chunk):
                m = mass[k, x - 2]
                fresh[k, x] = jnp.where(n > k, keep * m + add, m)
            return 0

        lax.fori_loop(2, X, inner, 0)
        span = pl.ds(i * chunk, chunk)
        stores.append(pltpu.make_async_copy(fresh.at[span], mass_out.at[span], out_sem.at[i]))
        stores[-1].start()
    for c in moves + stores:
        c.wait()


def local(tun_size, sec_size, wind, heat, soot, mass, count, label, onset):
    slots, X, Y, Z = mass.shape
    f32 = jnp.float32
    any_spec = pl.BlockSpec(memory_space=pl.ANY)
    vmem_spec = pl.BlockSpec(memory_space=pltpu.VMEM)
    state, coef, mass_in = pl.pallas_call(
        functools.partial(exchange_kernel, tun_size, sec_size),
        out_shape=(
            jax.ShapeDtypeStruct((FIELDS, X, Y, Z), f32),
            jax.ShapeDtypeStruct((3, X, Y, Z), f32),
            jax.ShapeDtypeStruct((slots, 2, Y, Z), f32),
        ),
        in_specs=[any_spec] * 6 + [pl.BlockSpec(memory_space=pltpu.SMEM)],
        out_specs=(vmem_spec,) * 3,
        scratch_shapes=[
            pltpu.VMEM((ALL, X + 4, Y + 8, Z), f32),
            pltpu.VMEM((FIELDS + 1, X + 2, Y + 8, Z), f32),
            pltpu.VMEM((X + 2, Y, Z), f32),
            pltpu.VMEM((X, Y, Z), f32),
            pltpu.VMEM((slots, X, Y, Z), f32),
            pltpu.VMEM((X, Y, Z), jnp.int32),
            pltpu.VMEM((X, Y, Z), jnp.int32),
            pltpu.VMEM((X, 2, 8, Z), f32),
            pltpu.VMEM((X, 2, 8, Z), f32),
            pltpu.VMEM((X + 2, 2, 8, Z), f32),
            pltpu.VMEM((X + 2, 2, 8, Z), f32),
            pltpu.SemaphoreType.DMA((6,)),
            pltpu.SemaphoreType.DMA((15,)),
            pltpu.SemaphoreType.DMA((15,)),
        ],
        compiler_params=pltpu.CompilerParams(
            collective_id=0, has_side_effects=True, vmem_limit_bytes=24 << 20
        ),
        name="fields",
    )(wind, heat, soot, mass, count, label, onset)
    parts = 4
    return pl.pallas_call(
        functools.partial(droplet_kernel, slots // parts),
        out_shape=(
            jax.ShapeDtypeStruct((3, X, Y, Z), f32),
            jax.ShapeDtypeStruct((X, Y, Z), f32),
            jax.ShapeDtypeStruct((X, Y, Z), f32),
            jax.ShapeDtypeStruct((slots, X, Y, Z), f32),
            jax.ShapeDtypeStruct((X, Y, Z), jnp.int32),
        ),
        in_specs=[any_spec, any_spec, vmem_spec, vmem_spec],
        out_specs=(any_spec,) * 5,
        scratch_shapes=[
            pltpu.VMEM((slots, X - 2, Y, Z), f32),
            pltpu.VMEM((slots, X, Y, Z), f32),
            pltpu.VMEM((X, Y, Z), jnp.int32),
            pltpu.SemaphoreType.DMA((parts,)),
            pltpu.SemaphoreType.DMA((parts,)),
            pltpu.SemaphoreType.DMA((4,)),
        ],
        compiler_params=pltpu.CompilerParams(vmem_limit_bytes=24 << 20),
        name="droplets",
    )(mass, state, coef, mass_in)


def solution(mesh):
    return jax.shard_map(
        functools.partial(local, mesh.shape["tun"], mesh.shape["sec"]),
        mesh=mesh,
        in_specs=(
            P(None, "tun", "sec", None),
            P("tun", "sec", None),
            P("tun", "sec", None),
            P(None, "tun", "sec", None),
            P("tun", "sec", None),
            P("tun", "sec", None),
            P(),
        ),
        out_specs=(
            P(None, "tun", "sec", None),
            P("tun", "sec", None),
            P("tun", "sec", None),
            P(None, "tun", "sec", None),
            P("tun", "sec", None),
        ),
        check_vma=False,
    )
```

time: 97.6 us -> 20 us (0.20)
  starting transfers between devices: 76 us -> 0 us
  Pallas kernels: 0 us -> 12.8 us
  waiting for transfers between devices: 7.67 us -> 0 us
  other arithmetic: 6.55 us -> 0 us
  local copies, waits for them, and re-layouts: 4.69 us -> 6.16 us
    ppermute x26 -> x0, starting transfers between devices: 76 us -> none  [the longest x12 39.6 us: extended(): lax.ppermute(head, axis, [((i + 1) % count, i) for i in range(ends)])]
    pallas_call x0 -> x2, Pallas kernels: none -> 12.8 us  [the longest x1 11.4 us: local(): pl.pallas_call(functools.partial(exchange_kernel, tun_size, sec_size), ou...]
    ppermute x26 -> x0, waiting for transfers between devices: 7.67 us -> none  [the longest x12 7.63 us: extended(): lax.ppermute(head, axis, [((i + 1) % count, i) for i in range(ends)])]
    unnamed x21 -> x16, local copies, waits for them, and re-layouts: 1.37 us -> 6.16 us
    slice x10 -> x0, local copies, waits for them, and re-layouts: 2.36 us -> none  [the longest x3 2.24 us: extended(): head = lax.slice_in_dim(cells, 0, width, axis=dim)]
    mul x7 -> x0, other arithmetic: 1.63 us -> none  [the longest x2 0.97 us: advance(): advection = advection + 0.5 * centre[dim] * (upper - lower)]
    convert_element_type x4 -> x0, other arithmetic: 1.39 us -> none  [the longest x1 0.72 us: local(): count[-1][None].astype(jnp.float32)]
  transfers between devices with their start and end apart: 26 -> 0, of which waited for: 3 -> 0; matrix products, arithmetic and copies ran while one was open for 8% -> 0% of each run, Pallas kernels for 0% -> 0%
where the time goes in v1:
time: 20 us; the launch traced here: 19.6 us
  Pallas kernels  12.8 us (64%)
  local copies, waits for them, and re-layouts  6.16 us (31%)
  between operations  0.66 us (3%)
    pallas_call x1, Pallas kernels, local(): pl.pallas_call(functools.partial(exchange_kernel, tun_size, sec_size), ou...  11.4 us
    unnamed x16, local copies, waits for them, and re-layouts  6.16 us
    pallas_call x1, Pallas kernels, local(): pl.pallas_call(functools.partial(droplet_kernel, slots // parts), out_sha...  1.45 us

profile of v1, /device:TPU:12, one launch (start us, length us, event | category | flops | bytes accessed | tf_op | source)
XLA Modules:
  0.0 19.6 jit_solution(16978157144567189253)
XLA Ops:
  0.6 0.0 copy-start
  0.6 1.2 %copy-done = f32[16,8,16,128]{3,2,1,0:T(8,128)S(1)} copy-done((f32[16,8,16,128]{3,2,1,0:T(8,128)S(1)}, f32[16,8,16,128]{3,2,1,0:T(8,128)}, u32[]{:S(2)}) %copy-start) | copy-done | bytes 1048600
  1.9 0.0 copy-start.2
  1.9 0.9 %copy-done.2 = f32[3,8,16,128]{3,2,1,0:T(8,128)S(1)} copy-done((f32[3,8,16,128]{3,2,1,0:T(8,128)S(1)}, f32[3,8,16,128]{3,2,1,0:T(8,128)}, u32[]{:S(2)}) %copy-start.2) | copy-done | bytes 196632
  2.8 0.0 copy-start.3
  2.8 0.8 %copy-done.3 = f32[8,16,128]{2,1,0:T(8,128)S(1)} copy-done((f32[8,16,128]{2,1,0:T(8,128)S(1)}, f32[8,16,128]{2,1,0:T(8,128)}, u32[]{:S(2)}) %copy-start.3) | copy-done | bytes 65560
  3.6 0.0 copy-start.4
  3.6 0.8 %copy-done.4 = f32[8,16,128]{2,1,0:T(8,128)S(1)} copy-done((f32[8,16,128]{2,1,0:T(8,128)S(1)}, f32[8,16,128]{2,1,0:T(8,128)}, u32[]{:S(2)}) %copy-start.4) | copy-done | bytes 65560
  4.5 0.0 copy-start.5
  4.5 0.8 %copy-done.5 = s32[8,16,128]{2,1,0:T(8,128)S(1)} copy-done((s32[8,16,128]{2,1,0:T(8,128)S(1)}, s32[8,16,128]{2,1,0:T(8,128)}, u32[]{:S(2)}) %copy-start.5) | copy-done | bytes 65560
  5.3 0.0 copy-start.6
  5.3 0.8 %copy-done.6 = s32[8,16,128]{2,1,0:T(8,128)S(1)} copy-done((s32[8,16,128]{2,1,0:T(8,128)S(1)}, s32[8,16,128]{2,1,0:T(8,128)}, u32[]{:S(2)}) %copy-start.6) | copy-done | bytes 65560
  6.1 0.0 copy-start.7
  6.1 0.7 %copy-done.7 = s32[8]{0:T(128)S(1)} copy-done((s32[8]{0:T(128)S(1)}, s32[8]{0:T(128)}, u32[]{:S(2)}) %copy-start.7) | copy-done | bytes 56
  6.8 0.0 copy-start.1
  6.8 11.4 %fields.1 = (f32[5,8,16,128]{3,2,1,0:T(8,128)S(1)}, f32[3,8,16,128]{3,2,1,0:T(8,128)S(1)}, f32[16,2,16,128]{3,2,1,0:T(8,128)S(1)}) custom-call(f32[3,8,16,128]{3,2,1,0:T(8,128)S(1)} %copy-done.2, f32[8,16,128]{2,1,0:T(8,128)S(1)} %copy-done.3, f32[8,16,128]{2,1,0:T(8,128)S(1)} %copy-done.4, f32[16,8,16,128]{3,2,1,0:T(8,128)S(1)} %copy-done, ...), custom_call_target="tpu_custom_call" | custom-call | tf_op jit(solution)/shard_map/fields/pallas_call | solution.py:368
  18.2 0.0 copy-done.1
  18.2 1.4 %droplets.1 = (f32[3,8,16,128]{3,2,1,0:T(8,128)}, f32[8,16,128]{2,1,0:T(8,128)}, f32[8,16,128]{2,1,0:T(8,128)}, f32[16,8,16,128]{3,2,1,0:T(8,128)}, s32[8,16,128]{2,1,0:T(8,128)}) custom-call(f32[16,8,16,128]{3,2,1,0:T(8,128)S(1)} %copy-done.1, f32[5,8,16,128]{3,2,1,0:T(8,128)S(1)} %get-tuple-element.8.state, f32[3,8,16,128]{3,2,1,0:T(8,128)S(1)} %get-tuple-element.9.coef, ...), custom_call_target="tpu_custom_call" | custom-call | tf_op jit(solution)/shard_map/droplets/pallas_call | solution.py:399
Async XLA Ops:
  0.6 1.2 %copy-start = (f32[16,8,16,128]{3,2,1,0:T(8,128)S(1)}, f32[16,8,16,128]{3,2,1,0:T(8,128)}, u32[]{:S(2)}) copy-start(f32[16,8,16,128]{3,2,1,0:T(8,128)} %mass_hbm.3) | copy-start | bytes 3145732
  1.9 0.9 %copy-start.2 = (f32[3,8,16,128]{3,2,1,0:T(8,128)S(1)}, f32[3,8,16,128]{3,2,1,0:T(8,128)}, u32[]{:S(2)}) copy-start(f32[3,8,16,128]{3,2,1,0:T(8,128)} %wind_hbm.1) | copy-start | bytes 589828
  2.8 0.8 %copy-start.3 = (f32[8,16,128]{2,1,0:T(8,128)S(1)}, f32[8,16,128]{2,1,0:T(8,128)}, u32[]{:S(2)}) copy-start(f32[8,16,128]{2,1,0:T(8,128)} %heat_hbm.1) | copy-start | bytes 196612
  3.6 0.8 %copy-start.4 = (f32[8,16,128]{2,1,0:T(8,128)S(1)}, f32[8,16,128]{2,1,0:T(8,128)}, u32[]{:S(2)}) copy-start(f32[8,16,128]{2,1,0:T(8,128)} %soot_hbm.1) | copy-start | bytes 196612
  4.5 0.8 %copy-start.5 = (s32[8,16,128]{2,1,0:T(8,128)S(1)}, s32[8,16,128]{2,1,0:T(8,128)}, u32[]{:S(2)}) copy-start(s32[8,16,128]{2,1,0:T(8,128)} %count_hbm.1) | copy-start | bytes 196612
  5.3 0.8 %copy-start.6 = (s32[8,16,128]{2,1,0:T(8,128)S(1)}, s32[8,16,128]{2,1,0:T(8,128)}, u32[]{:S(2)}) copy-start(s32[8,16,128]{2,1,0:T(8,128)} %label_hbm.1) | copy-start | bytes 196612
  6.1 0.7 %copy-start.7 = (s32[8]{0:T(128)S(1)}, s32[8]{0:T(128)}, u32[]{:S(2)}) copy-start(s32[8]{0:T(128)} %onset.1) | copy-start | bytes 100
  6.8 11.4 %copy-start.1 = (f32[16,8,16,128]{3,2,1,0:T(8,128)S(1)}, f32[16,8,16,128]{3,2,1,0:T(8,128)}, u32[]{:S(2)}) copy-start(f32[16,8,16,128]{3,2,1,0:T(8,128)} %mass_hbm.3) | copy-start | bytes 3145732

commit v2 on v1

--- a/solution.py
+++ b/solution.py
@@ -72,9 +72,9 @@
 
 def exchange_kernel(
     tun_size, sec_size,
-    wind_hbm, heat_hbm, soot_hbm, mass_hbm, count_hbm, label_hbm, onset,
+    wind_hbm, heat_hbm, soot_hbm, mass_hbm, count_hbm, label_hbm, onset_hbm,
     state, coef, mass_in,
-    ext, first, kept_first, spray_next, mass, count, label,
+    ext, first, kept_first, spray_next, mass, count, label, onset,
     pack_low, pack_high, from_low, from_high,
     local_sem, send_sem, recv_sem,
 ):
@@ -91,20 +91,6 @@
 
     around = [(a, b) for a in (-1, 0, 1) for b in (-1, 0, 1) if a or b]
 
-    def load(i, src, dst):
-        return pltpu.make_async_copy(src, dst, local_sem.at[i])
-
-    loads = [
-        load(0, count_hbm, count),
-        load(1, label_hbm, label),
-        load(2, mass_hbm, mass),
-        load(3, wind_hbm, ext.at[0:3, 2:X + 2, 0:Y]),
-        load(4, heat_hbm, ext.at[3, 2:X + 2, 0:Y]),
-        load(5, soot_hbm, ext.at[4, 2:X + 2, 0:Y]),
-    ]
-    for c in loads:
-        c.start()
-
     barrier = pltpu.get_barrier_semaphore()
     for a, b in around:
         @pl.when(exists(a, b))
@@ -112,6 +98,49 @@
             pl.semaphore_signal(
                 barrier, inc=1, device_id={"tun": t + a, "sec": s + b}, device_id_type=MESH
             )
+
+    def load(i, src, dst):
+        return pltpu.make_async_copy(src, dst, local_sem.at[i])
+
+    loads = [
+        load(0, wind_hbm, ext.at[0:3, 2:X + 2, 0:Y]),
+        load(1, heat_hbm, ext.at[3, 2:X + 2, 0:Y]),
+        load(2, soot_hbm, ext.at[4, 2:X + 2, 0:Y]),
+        load(3, count_hbm, count),
+        load(4, mass_hbm, mass),
+        load(5, label_hbm, label),
+        load(6, onset_hbm, onset),
+    ]
+    for c in loads:
+        c.start()
+
+    row = lax.broadcasted_iota(jnp.int32, (8, Z), 0)
+
+    def pack(g):
+        def one(x, _):
+            low = high = None
+            for j in range(4):
+                f = 4 * g + j
+                tile_low = ext[f, x + 2, 0:8]
+                tile_high = ext[f, x + 2, Y - 8:Y]
+                if j == 0:
+                    low, high = tile_low, tile_high
+                else:
+                    here = jnp.logical_and(row >= 2 * j, row < 2 * j + 2)
+                    low = jnp.where(here, pltpu.roll(tile_low, 2 * j, 0), low)
+                    place = (2 * j + 6) % 8
+                    there = jnp.logical_and(row >= place, row < place + 2)
+                    high = jnp.where(there, pltpu.roll(tile_high, 2 * j, 0), high)
+            pack_low[g, x] = low
+            pack_high[g, x] = high
+            return 0
+
+        lax.fori_loop(0, X, one, 0, unroll=2)
+
+    for c in loads[:3]:
+        c.wait()
+    pack(0)
+
     wide = has[-1].astype(jnp.int32) + has[1].astype(jnp.int32)
     deep = has_sec[-1].astype(jnp.int32) + has_sec[1].astype(jnp.int32)
     pl.semaphore_wait(barrier, (1 + wide) * (1 + deep) - 1)
@@ -142,9 +171,14 @@
         send(4, -1, 0, heat_hbm.at[0:2], ext.at[3, X + 2:X + 4, 0:Y]),
         send(5, -1, 0, soot_hbm.at[0:2], ext.at[4, X + 2:X + 4, 0:Y]),
     ]
+    rows_first = [
+        send(8, 0, -1, pack_low.at[0], from_high.at[0, 1:X + 1]),
+        send(9, 0, 1, pack_high.at[0], from_low.at[0, 1:X + 1]),
+    ]
+    start(rows_first)
     start(fields)
 
-    for c in loads[:3]:
+    for c in loads[3:]:
         c.wait()
 
     def sums(x, _):
@@ -163,61 +197,38 @@
         spray_next[x] = jnp.where(onset_here <= 1, inject_rate, 0.0)
         return 0
 
-    lax.fori_loop(0, X, sums, 0)
+    lax.fori_loop(0, X, sums, 0, unroll=2)
     drops = [
         send(6, 1, 0, ext.at[LOAD:ALL, X:X + 2, 0:Y], ext.at[LOAD:ALL, 0:2, 0:Y]),
         send(7, -1, 0, ext.at[SPRAY, 2:4, 0:Y], ext.at[SPRAY, X + 2:X + 4, 0:Y]),
     ]
     start(drops)
-    for c in loads[3:]:
-        c.wait()
-
-    row = lax.broadcasted_iota(jnp.int32, (8, Z), 0)
-
-    def packing(x, _):
-        for g in range(2):
-            low = high = None
-            for j in range(4):
-                f = 4 * g + j
-                tile_low = ext[f, x + 2, 0:8]
-                tile_high = ext[f, x + 2, Y - 8:Y]
-                if j == 0:
-                    low, high = tile_low, tile_high
-                else:
-                    here = jnp.logical_and(row >= 2 * j, row < 2 * j + 2)
-                    low = jnp.where(here, pltpu.roll(tile_low, 2 * j, 0), low)
-                    place = (2 * j + 6) % 8
-                    there = jnp.logical_and(row >= place, row < place + 2)
-                    high = jnp.where(there, pltpu.roll(tile_high, 2 * j, 0), high)
-            pack_low[x, g] = low
-            pack_high[x, g] = high
-        return 0
-
-    lax.fori_loop(0, X, packing, 0)
+
+    pack(1)
     across = [
-        send(8, 0, -1, pack_low, from_high.at[1:X + 1]),
-        send(9, 0, 1, pack_high, from_low.at[1:X + 1]),
-        send(10, -1, -1, pack_low.at[0], from_high.at[X + 1]),
-        send(11, 1, -1, pack_low.at[X - 1], from_high.at[0]),
-        send(12, -1, 1, pack_high.at[0], from_low.at[X + 1]),
-        send(13, 1, 1, pack_high.at[X - 1], from_low.at[0]),
+        send(10, 0, -1, pack_low.at[1], from_high.at[1, 1:X + 1]),
+        send(11, 0, 1, pack_high.at[1], from_low.at[1, 1:X + 1]),
+        send(12, -1, -1, pack_low.at[:, 0], from_high.at[:, X + 1]),
+        send(13, 1, -1, pack_low.at[:, X - 1], from_high.at[:, 0]),
+        send(14, -1, 1, pack_high.at[:, 0], from_low.at[:, X + 1]),
+        send(15, 1, 1, pack_high.at[:, X - 1], from_low.at[:, 0]),
     ]
     start(across)
-    masses = [send(14, 1, 0, mass_hbm.at[:, X - 2:X], mass_in)]
+    masses = [send(16, 1, 0, mass_hbm.at[:, X - 2:X], mass_in)]
     start(masses)
 
     @pl.when(jnp.logical_not(has[-1]))
     def _():
         ext[:, 0:2] = jnp.zeros((ALL, 2) + ext.shape[2:], jnp.float32)
-        from_low[0] = jnp.zeros(from_low.shape[1:], jnp.float32)
-        from_high[0] = jnp.zeros(from_low.shape[1:], jnp.float32)
+        from_low[:, 0] = jnp.zeros((2, 8, Z), jnp.float32)
+        from_high[:, 0] = jnp.zeros((2, 8, Z), jnp.float32)
         mass_in[...] = jnp.zeros(mass_in.shape, jnp.float32)
 
     @pl.when(jnp.logical_not(has[1]))
     def _():
         ext[:, X + 2:X + 4] = jnp.zeros((ALL, 2) + ext.shape[2:], jnp.float32)
-        from_low[X + 1] = jnp.zeros(from_low.shape[1:], jnp.float32)
-        from_high[X + 1] = jnp.zeros(from_low.shape[1:], jnp.float32)
+        from_low[:, X + 1] = jnp.zeros((2, 8, Z), jnp.float32)
+        from_high[:, X + 1] = jnp.zeros((2, 8, Z), jnp.float32)
 
     @pl.when(jnp.logical_not(has_sec[-1]))
     def _():
@@ -227,20 +238,20 @@
     def _():
         from_high[...] = jnp.zeros(from_high.shape, jnp.float32)
 
-    wait_recv(fields + drops + across)
+    wait_recv(rows_first + fields + drops + across)
 
     def unpacking(p, _):
         for g in range(2):
-            high, low = from_high[p], from_low[p]
+            high, low = from_high[g, p], from_low[g, p]
             for j in range(4):
                 here = jnp.logical_and(row >= 2 * j, row < 2 * j + 2)
-                tile = jnp.where(here, high[g], low[g])
+                tile = jnp.where(here, high, low)
                 if j:
                     tile = pltpu.roll(tile, 8 - 2 * j, 0)
                 ext[4 * g + j, p + 1, Y:Y + 8] = tile
         return 0
 
-    lax.fori_loop(0, X + 2, unpacking, 0)
+    lax.fori_loop(0, X + 2, unpacking, 0, unroll=2)
 
     lane = lax.broadcasted_iota(jnp.int32, (Y + 8, Z), 1)
 
@@ -300,28 +311,19 @@
     lax.fori_loop(1, X + 1, substep_second, (jnp.tanh(first[3, 0]), jnp.tanh(first[3, 1])))
 
     wait_recv(masses)
-    for a, b, copy in fields + drops + across + masses:
+    for a, b, copy in rows_first + fields + drops + across + masses:
         @pl.when(exists(a, b))
         def _(copy=copy):
             copy.wait_send()
 
 
 def droplet_kernel(
-    chunk, mass_hbm, state, coef, mass_in,
+    chunk, mass, state, coef, mass_in,
     wind_out, heat_out, soot_out, mass_out, count_out,
-    mass, fresh, tally, in_sem, out_sem, state_sem,
+    fresh, tally, out_sem, state_sem,
 ):
-    slots, X = mass_hbm.shape[:2]
+    slots, X = mass.shape[:2]
     parts = slots // chunk
-    loads = [
-        pltpu.make_async_copy(
-            mass_hbm.at[pl.ds(i * chunk, chunk), 0:X - 2], mass.at[pl.ds(i * chunk, chunk)],
-            in_sem.at[i],
-        )
-        for i in range(parts)
-    ]
-    for c in loads:
-        c.start()
     moves = [
         pltpu.make_async_copy(state.at[0:3], wind_out, state_sem.at[0]),
         pltpu.make_async_copy(state.at[3], heat_out, state_sem.at[1]),
@@ -343,8 +345,6 @@
                 return 0
 
             lax.fori_loop(0, 2, edge, 0)
-        loads[i].wait()
-
         def inner(x, _, i=i):
             keep, add, n = coef[0, x], coef[1, x], coef[2, x]
             for k in range(i * chunk, (i + 1) * chunk):
@@ -372,7 +372,7 @@
             jax.ShapeDtypeStruct((3, X, Y, Z), f32),
             jax.ShapeDtypeStruct((slots, 2, Y, Z), f32),
         ),
-        in_specs=[any_spec] * 6 + [pl.BlockSpec(memory_space=pltpu.SMEM)],
+        in_specs=[pl.BlockSpec(memory_space=pltpu.HBM)] * 7,
         out_specs=(vmem_spec,) * 3,
         scratch_shapes=[
             pltpu.VMEM((ALL, X + 4, Y + 8, Z), f32),
@@ -382,19 +382,23 @@
             pltpu.VMEM((slots, X, Y, Z), f32),
             pltpu.VMEM((X, Y, Z), jnp.int32),
             pltpu.VMEM((X, Y, Z), jnp.int32),
-            pltpu.VMEM((X, 2, 8, Z), f32),
-            pltpu.VMEM((X, 2, 8, Z), f32),
-            pltpu.VMEM((X + 2, 2, 8, Z), f32),
-            pltpu.VMEM((X + 2, 2, 8, Z), f32),
-            pltpu.SemaphoreType.DMA((6,)),
-            pltpu.SemaphoreType.DMA((15,)),
-            pltpu.SemaphoreType.DMA((15,)),
+            pltpu.SMEM(onset.shape, jnp.int32),
+            pltpu.VMEM((2, X, 8, Z), f32),
+            pltpu.VMEM((2, X, 8, Z), f32),
+            pltpu.VMEM((2, X + 2, 8, Z), f32),
+            pltpu.VMEM((2, X + 2, 8, Z), f32),
+            pltpu.SemaphoreType.DMA((7,)),
+            pltpu.SemaphoreType.DMA((17,)),
+            pltpu.SemaphoreType.DMA((17,)),
         ],
         compiler_params=pltpu.CompilerParams(
             collective_id=0, has_side_effects=True, vmem_limit_bytes=24 << 20
         ),
         name="fields",
-    )(wind, heat, soot, mass, count, label, onset)
+    )(*[
+        pltpu.with_memory_space_constraint(a, pltpu.HBM)
+        for a in (wind, heat, soot, mass, count, label, onset)
+    ])
     parts = 4
     return pl.pallas_call(
         functools.partial(droplet_kernel, slots // parts),
@@ -405,13 +409,11 @@
             jax.ShapeDtypeStruct((slots, X, Y, Z), f32),
             jax.ShapeDtypeStruct((X, Y, Z), jnp.int32),
         ),
-        in_specs=[any_spec, any_spec, vmem_spec, vmem_spec],
+        in_specs=[vmem_spec, any_spec, vmem_spec, vmem_spec],
         out_specs=(any_spec,) * 5,
         scratch_shapes=[
-            pltpu.VMEM((slots, X - 2, Y, Z), f32),
             pltpu.VMEM((slots, X, Y, Z), f32),
             pltpu.VMEM((X, Y, Z), jnp.int32),
-            pltpu.SemaphoreType.DMA((parts,)),
             pltpu.SemaphoreType.DMA((parts,)),
             pltpu.SemaphoreType.DMA((4,)),
         ],

time: 20 us -> 12.8 us (0.64); the launches traced: 19.6 us -> 12.7 us
  local copies, waits for them, and re-layouts: 6.16 us -> 0.01 us
  Pallas kernels: 12.8 us -> 12 us
    unnamed x16 -> x2, local copies, waits for them, and re-layouts: 6.16 us -> 0.01 us
    pallas_call x1, Pallas kernels: 11.4 us -> 10.8 us  [local(): pl.pallas_call(functools.partial(exchange_kernel, tun_size, sec_size), ou...]
    pallas_call x1, Pallas kernels: 1.45 us -> 1.16 us  [local(): pl.pallas_call(functools.partial(droplet_kernel, slots // parts), out_sha...]
where the time goes in v2:
time: 12.8 us; the launch traced here: 12.7 us
  Pallas kernels  12 us (94%)
  between operations  0.66 us (5%)
    pallas_call x1, Pallas kernels, local(): pl.pallas_call(functools.partial(exchange_kernel, tun_size, sec_size), ou...  10.8 us
    pallas_call x1, Pallas kernels, local(): pl.pallas_call(functools.partial(droplet_kernel, slots // parts), out_sha...  1.16 us

profile of v2, /device:TPU:12, one launch (start us, length us, event | category | flops | bytes accessed | tf_op | source)
XLA Modules:
  0.0 12.7 jit_solution(680157739435374627)
XLA Ops:
  0.6 0.0 copy-start
  0.6 10.8 %fields.1 = (f32[5,8,16,128]{3,2,1,0:T(8,128)S(1)}, f32[3,8,16,128]{3,2,1,0:T(8,128)S(1)}, f32[16,2,16,128]{3,2,1,0:T(8,128)S(1)}) custom-call(f32[3,8,16,128]{3,2,1,0:T(8,128)} %wind_hbm.1, f32[8,16,128]{2,1,0:T(8,128)} %heat_hbm.1, f32[8,16,128]{2,1,0:T(8,128)} %soot_hbm.1, f32[16,8,16,128]{3,2,1,0:T(8,128)} %mass.1, s32[8,16,128]{2,1,0:T(8,128)} %count_hbm.1, ...), custom_call_target="tpu_custom_call" | custom-call | tf_op jit(solution)/shard_map/fields/pallas_call | solution.py:368
  11.5 0.0 copy-done
  11.5 1.2 %droplets.1 = (f32[3,8,16,128]{3,2,1,0:T(8,128)}, f32[8,16,128]{2,1,0:T(8,128)}, f32[8,16,128]{2,1,0:T(8,128)}, f32[16,8,16,128]{3,2,1,0:T(8,128)}, s32[8,16,128]{2,1,0:T(8,128)}) custom-call(f32[16,8,16,128]{3,2,1,0:T(8,128)S(1)} %copy-done, f32[5,8,16,128]{3,2,1,0:T(8,128)S(1)} %get-tuple-element.8.state, f32[3,8,16,128]{3,2,1,0:T(8,128)S(1)} %get-tuple-element.9.coef, ...), custom_call_target="tpu_custom_call" | custom-call | tf_op jit(solution)/shard_map/droplets/pallas_call | solution.py:403
Async XLA Ops:
  0.6 10.9 %copy-start = (f32[16,8,16,128]{3,2,1,0:T(8,128)S(1)}, f32[16,8,16,128]{3,2,1,0:T(8,128)}, u32[]{:S(2)}) copy-start(f32[16,8,16,128]{3,2,1,0:T(8,128)} %mass.1) | copy-start | bytes 3145732

commit v3 on v2

--- a/solution.py
+++ b/solution.py
@@ -73,8 +73,8 @@
 def exchange_kernel(
     tun_size, sec_size,
     wind_hbm, heat_hbm, soot_hbm, mass_hbm, count_hbm, label_hbm, onset_hbm,
-    state, coef, mass_in,
-    ext, first, kept_first, spray_next, mass, count, label, onset,
+    state, fresh_mass, tally_out,
+    ext, first, kept_first, spray_next, mass, count, label, onset, coef, mass_in,
     pack_low, pack_high, from_low, from_high,
     local_sem, send_sem, recv_sem,
 ):
@@ -177,6 +177,8 @@
     ]
     start(rows_first)
     start(fields)
+    masses = [send(16, 1, 0, mass_hbm.at[:, X - 2:X], mass_in)]
+    start(masses)
 
     for c in loads[3:]:
         c.wait()
@@ -214,8 +216,6 @@
         send(15, 1, 1, pack_high.at[:, X - 1], from_low.at[:, 0]),
     ]
     start(across)
-    masses = [send(16, 1, 0, mass_hbm.at[:, X - 2:X], mass_in)]
-    start(masses)
 
     @pl.when(jnp.logical_not(has[-1]))
     def _():
@@ -238,7 +238,7 @@
     def _():
         from_high[...] = jnp.zeros(from_high.shape, jnp.float32)
 
-    wait_recv(rows_first + fields + drops + across)
+    wait_recv(rows_first + fields[3:] + drops[1:] + across[:2] + [across[2], across[4]])
 
     def unpacking(p, _):
         for g in range(2):
@@ -251,7 +251,7 @@
                 ext[4 * g + j, p + 1, Y:Y + 8] = tile
         return 0
 
-    lax.fori_loop(0, X + 2, unpacking, 0, unroll=2)
+    lax.fori_loop(1, X + 2, unpacking, 0, unroll=3)
 
     lane = lax.broadcasted_iota(jnp.int32, (Y + 8, Z), 1)
 
@@ -270,23 +270,19 @@
         kept_first[p - 1] = kept[:Y]
         return th, th_ahead
 
-    lax.fori_loop(1, X + 3, substep_first, (jnp.tanh(ext[3, 0]), jnp.tanh(ext[3, 1])))
-
-    @pl.when(jnp.logical_not(has[-1]))
-    def _():
-        first[:, 0] = jnp.zeros((first.shape[0],) + first.shape[2:], jnp.float32)
-
-    @pl.when(jnp.logical_not(has[1]))
-    def _():
-        first[:, X + 1] = jnp.zeros((first.shape[0],) + first.shape[2:], jnp.float32)
-
-    @pl.when(jnp.logical_not(has_sec[-1]))
-    def _():
-        first[:, :, Y + 7:Y + 8] = jnp.zeros(first.shape[:2] + (1, Z), jnp.float32)
-
-    @pl.when(jnp.logical_not(has_sec[1]))
-    def _():
-        first[:, :, Y:Y + 1] = jnp.zeros(first.shape[:2] + (1, Z), jnp.float32)
+    def first_planes(low, high):
+        start_th = (jnp.tanh(ext[3, low - 1]), jnp.tanh(ext[3, low]))
+        lax.fori_loop(low, high, substep_first, start_th, unroll=2)
+
+        @pl.when(jnp.logical_not(has_sec[-1]))
+        def _():
+            first[:, low - 1:high - 1, Y + 7:Y + 8] = jnp.zeros(
+                (FIELDS + 1, high - low, 1, Z), jnp.float32)
+
+        @pl.when(jnp.logical_not(has_sec[1]))
+        def _():
+            first[:, low - 1:high - 1, Y:Y + 1] = jnp.zeros(
+                (FIELDS + 1, high - low, 1, Z), jnp.float32)
 
     def substep_second(p, carry):
         th_behind, th = carry
@@ -303,60 +299,66 @@
         for f in range(FIELDS):
             state[f, x] = fresh[f]
         before = kept_first[p - 1]
-        coef[0, x] = before * kept
-        coef[1, x] = (ext[SPRAY, x + 1, 0:Y] * before + spray) * kept
-        coef[2, x] = tally
+        keep, add = before * kept, (ext[SPRAY, x + 1, 0:Y] * before + spray) * kept
+        n = tally.astype(jnp.int32)
+        tally_out[x] = n
+        return keep, add, n, th, th_ahead
+
+    def slot_masses(x, keep, add, n, source, plane):
+        for k in range(slots):
+            m = source[k, plane]
+            fresh_mass[k, x] = jnp.where(n > k, keep * m + add, m)
+
+    def upper(p, carry):
+        keep, add, n, th, th_ahead = substep_second(p, carry)
+        slot_masses(p - 1, keep, add, n, mass, p - 3)
         return th, th_ahead
 
-    lax.fori_loop(1, X + 1, substep_second, (jnp.tanh(first[3, 0]), jnp.tanh(first[3, 1])))
-
+    def lowest(p, carry):
+        keep, add, n, th, th_ahead = substep_second(p, carry)
+        coef[0, p - 1], coef[1, p - 1] = keep, add
+        return th, th_ahead
+
+    first_planes(3, X + 3)
+
+    @pl.when(jnp.logical_not(has[1]))
+    def _():
+        first[:, X + 1] = jnp.zeros((FIELDS + 1, Y + 8, Z), jnp.float32)
+
+    lax.fori_loop(3, X + 1, upper, (jnp.tanh(first[3, 2]), jnp.tanh(first[3, 3])), unroll=2)
+
+    wait_recv(fields[:3] + drops[:1] + [across[3], across[5]])
+    unpacking(0, 0)
+    first_planes(1, 3)
+
+    @pl.when(jnp.logical_not(has[-1]))
+    def _():
+        first[:, 0] = jnp.zeros((FIELDS + 1, Y + 8, Z), jnp.float32)
+
+    lax.fori_loop(1, 3, lowest, (jnp.tanh(first[3, 0]), jnp.tanh(first[3, 1])), unroll=2)
     wait_recv(masses)
+    for x in range(2):
+        slot_masses(x, coef[0, x], coef[1, x], tally_out[x], mass_in, x)
     for a, b, copy in rows_first + fields + drops + across + masses:
         @pl.when(exists(a, b))
         def _(copy=copy):
             copy.wait_send()
 
 
-def droplet_kernel(
-    chunk, mass, state, coef, mass_in,
-    wind_out, heat_out, soot_out, mass_out, count_out,
-    fresh, tally, out_sem, state_sem,
-):
-    slots, X = mass.shape[:2]
-    parts = slots // chunk
-    moves = [
-        pltpu.make_async_copy(state.at[0:3], wind_out, state_sem.at[0]),
-        pltpu.make_async_copy(state.at[3], heat_out, state_sem.at[1]),
-        pltpu.make_async_copy(state.at[4], soot_out, state_sem.at[2]),
-        pltpu.make_async_copy(tally, count_out, state_sem.at[3]),
-    ]
-    for c in moves[:3]:
+def output_kernel(state, mass, tally, wind_out, heat_out, soot_out, mass_out, count_out, sem):
+    copies = [
+        pltpu.make_async_copy(src, dst, sem.at[i])
+        for i, (src, dst) in enumerate([
+            (mass, mass_out),
+            (state.at[0:3], wind_out),
+            (state.at[3], heat_out),
+            (state.at[4], soot_out),
+            (tally, count_out),
+        ])
+    ]
+    for c in copies:
         c.start()
-    tally[...] = coef[2].astype(jnp.int32)
-    moves[3].start()
-    stores = []
-    for i in range(parts):
-        if i == 0:
-            def edge(x, _):
-                keep, add, n = coef[0, x], coef[1, x], coef[2, x]
-                for k in range(slots):
-                    m = mass_in[k, x]
-                    fresh[k, x] = jnp.where(n > k, keep * m + add, m)
-                return 0
-
-            lax.fori_loop(0, 2, edge, 0)
-        def inner(x, _, i=i):
-            keep, add, n = coef[0, x], coef[1, x], coef[2, x]
-            for k in range(i * chunk, (i + 1) * chunk):
-                m = mass[k, x - 2]
-                fresh[k, x] = jnp.where(n > k, keep * m + add, m)
-            return 0
-
-        lax.fori_loop(2, X, inner, 0)
-        span = pl.ds(i * chunk, chunk)
-        stores.append(pltpu.make_async_copy(fresh.at[span], mass_out.at[span], out_sem.at[i]))
-        stores[-1].start()
-    for c in moves + stores:
+    for c in copies:
         c.wait()
 
 
@@ -365,12 +367,12 @@
     f32 = jnp.float32
     any_spec = pl.BlockSpec(memory_space=pl.ANY)
     vmem_spec = pl.BlockSpec(memory_space=pltpu.VMEM)
-    state, coef, mass_in = pl.pallas_call(
+    state, fresh_mass, tally = pl.pallas_call(
         functools.partial(exchange_kernel, tun_size, sec_size),
         out_shape=(
             jax.ShapeDtypeStruct((FIELDS, X, Y, Z), f32),
-            jax.ShapeDtypeStruct((3, X, Y, Z), f32),
-            jax.ShapeDtypeStruct((slots, 2, Y, Z), f32),
+            jax.ShapeDtypeStruct((slots, X, Y, Z), f32),
+            jax.ShapeDtypeStruct((X, Y, Z), jnp.int32),
         ),
         in_specs=[pl.BlockSpec(memory_space=pltpu.HBM)] * 7,
         out_specs=(vmem_spec,) * 3,
@@ -383,6 +385,8 @@
             pltpu.VMEM((X, Y, Z), jnp.int32),
             pltpu.VMEM((X, Y, Z), jnp.int32),
             pltpu.SMEM(onset.shape, jnp.int32),
+            pltpu.VMEM((2, 2, Y, Z), f32),
+            pltpu.VMEM((slots, 2, Y, Z), f32),
             pltpu.VMEM((2, X, 8, Z), f32),
             pltpu.VMEM((2, X, 8, Z), f32),
             pltpu.VMEM((2, X + 2, 8, Z), f32),
@@ -399,9 +403,8 @@
         pltpu.with_memory_space_constraint(a, pltpu.HBM)
         for a in (wind, heat, soot, mass, count, label, onset)
     ])
-    parts = 4
     return pl.pallas_call(
-        functools.partial(droplet_kernel, slots // parts),
+        output_kernel,
         out_shape=(
             jax.ShapeDtypeStruct((3, X, Y, Z), f32),
             jax.ShapeDtypeStruct((X, Y, Z), f32),
@@ -409,17 +412,12 @@
             jax.ShapeDtypeStruct((slots, X, Y, Z), f32),
             jax.ShapeDtypeStruct((X, Y, Z), jnp.int32),
         ),
-        in_specs=[vmem_spec, any_spec, vmem_spec, vmem_spec],
+        in_specs=[vmem_spec] * 3,
         out_specs=(any_spec,) * 5,
-        scratch_shapes=[
-            pltpu.VMEM((slots, X, Y, Z), f32),
-            pltpu.VMEM((X, Y, Z), jnp.int32),
-            pltpu.SemaphoreType.DMA((parts,)),
-            pltpu.SemaphoreType.DMA((4,)),
-        ],
+        scratch_shapes=[pltpu.SemaphoreType.DMA((5,))],
         compiler_params=pltpu.CompilerParams(vmem_limit_bytes=24 << 20),
-        name="droplets",
-    )(mass, state, coef, mass_in)
+        name="outputs",
+    )(state, fresh_mass, tally)
 
 
 def solution(mesh):

time: 12.8 us -> 13.1 us (1.023)
  Pallas kernels: 12 us -> 12.3 us
    pallas_call x1, Pallas kernels: 10.8 us -> 11.2 us  [local(): pl.pallas_call(functools.partial(exchange_kernel, tun_size, sec_size), ou...]
where the time goes in v3:
time: 13.1 us; the launch traced here: 12.9 us
  Pallas kernels  12.3 us (94%)
  between operations  0.64 us (5%)
    pallas_call x1, Pallas kernels, local(): pl.pallas_call(functools.partial(exchange_kernel, tun_size, sec_size), ou...  11.2 us
    pallas_call x1, Pallas kernels, local(): pl.pallas_call(output_kernel, out_shape=(jax.ShapeDtypeStruct((3, X, Y, Z...  1.13 us

profile of v3, /device:TPU:12, one launch (start us, length us, event | category | flops | bytes accessed | tf_op | source)
XLA Modules:
  0.0 12.9 jit_solution(11087012710832622666)
XLA Ops:
  0.6 11.2 %fields.1 = (f32[5,8,16,128]{3,2,1,0:T(8,128)S(1)}, f32[16,8,16,128]{3,2,1,0:T(8,128)S(1)}, s32[8,16,128]{2,1,0:T(8,128)S(1)}) custom-call(f32[3,8,16,128]{3,2,1,0:T(8,128)} %wind_hbm.1, f32[8,16,128]{2,1,0:T(8,128)} %heat_hbm.1, f32[8,16,128]{2,1,0:T(8,128)} %soot_hbm.1, f32[16,8,16,128]{3,2,1,0:T(8,128)} %mass_hbm.1, s32[8,16,128]{2,1,0:T(8,128)} %count_hbm.1, ...), custom_call_target="tpu_custom_call" | custom-call | tf_op jit(solution)/shard_map/fields/pallas_call | solution.py:370
  11.8 1.1 %outputs.1 = (f32[3,8,16,128]{3,2,1,0:T(8,128)}, f32[8,16,128]{2,1,0:T(8,128)}, f32[8,16,128]{2,1,0:T(8,128)}, f32[16,8,16,128]{3,2,1,0:T(8,128)}, s32[8,16,128]{2,1,0:T(8,128)}) custom-call(f32[5,8,16,128]{3,2,1,0:T(8,128)S(1)} %get-tuple-element.8.state, f32[16,8,16,128]{3,2,1,0:T(8,128)S(1)} %get-tuple-element.9.mass, ...), custom_call_target="tpu_custom_call" | custom-call | tf_op jit(solution)/shard_map/outputs/pallas_call | solution.py:406

commit v4 on v3

--- a/solution.py
+++ b/solution.py
@@ -137,10 +137,6 @@
 
         lax.fori_loop(0, X, one, 0, unroll=2)
 
-    for c in loads[:3]:
-        c.wait()
-    pack(0)
-
     wide = has[-1].astype(jnp.int32) + has[1].astype(jnp.int32)
     deep = has_sec[-1].astype(jnp.int32) + has_sec[1].astype(jnp.int32)
     pl.semaphore_wait(barrier, (1 + wide) * (1 + deep) - 1)
@@ -171,14 +167,16 @@
         send(4, -1, 0, heat_hbm.at[0:2], ext.at[3, X + 2:X + 4, 0:Y]),
         send(5, -1, 0, soot_hbm.at[0:2], ext.at[4, X + 2:X + 4, 0:Y]),
     ]
+    start(fields)
+
+    for c in loads[:3]:
+        c.wait()
+    pack(0)
     rows_first = [
         send(8, 0, -1, pack_low.at[0], from_high.at[0, 1:X + 1]),
         send(9, 0, 1, pack_high.at[0], from_low.at[0, 1:X + 1]),
     ]
     start(rows_first)
-    start(fields)
-    masses = [send(16, 1, 0, mass_hbm.at[:, X - 2:X], mass_in)]
-    start(masses)
 
     for c in loads[3:]:
         c.wait()
@@ -201,10 +199,13 @@
 
     lax.fori_loop(0, X, sums, 0, unroll=2)
     drops = [
-        send(6, 1, 0, ext.at[LOAD:ALL, X:X + 2, 0:Y], ext.at[LOAD:ALL, 0:2, 0:Y]),
-        send(7, -1, 0, ext.at[SPRAY, 2:4, 0:Y], ext.at[SPRAY, X + 2:X + 4, 0:Y]),
+        send(6, 1, 0, ext.at[LOAD:SPRAY, X:X + 2, 0:Y], ext.at[LOAD:SPRAY, 0:2, 0:Y]),
+        send(7, 1, 0, ext.at[SPRAY, X + 1, 0:Y], ext.at[SPRAY, 1, 0:Y]),
+        send(17, -1, 0, ext.at[SPRAY, 2, 0:Y], ext.at[SPRAY, X + 2, 0:Y]),
     ]
     start(drops)
+    masses = [send(16, 1, 0, mass_hbm.at[:, X - 2:X], mass_in)]
+    start(masses)
 
     pack(1)
     across = [
@@ -238,7 +239,7 @@
     def _():
         from_high[...] = jnp.zeros(from_high.shape, jnp.float32)
 
-    wait_recv(rows_first + fields[3:] + drops[1:] + across[:2] + [across[2], across[4]])
+    wait_recv(rows_first + fields[3:] + drops[2:] + across[:2] + [across[2], across[4]])
 
     def unpacking(p, _):
         for g in range(2):
@@ -327,7 +328,7 @@
 
     lax.fori_loop(3, X + 1, upper, (jnp.tanh(first[3, 2]), jnp.tanh(first[3, 3])), unroll=2)
 
-    wait_recv(fields[:3] + drops[:1] + [across[3], across[5]])
+    wait_recv(fields[:3] + drops[:2] + [across[3], across[5]])
     unpacking(0, 0)
     first_planes(1, 3)
 
@@ -392,8 +393,8 @@
             pltpu.VMEM((2, X + 2, 8, Z), f32),
             pltpu.VMEM((2, X + 2, 8, Z), f32),
             pltpu.SemaphoreType.DMA((7,)),
-            pltpu.SemaphoreType.DMA((17,)),
-            pltpu.SemaphoreType.DMA((17,)),
+            pltpu.SemaphoreType.DMA((18,)),
+            pltpu.SemaphoreType.DMA((18,)),
         ],
         compiler_params=pltpu.CompilerParams(
             collective_id=0, has_side_effects=True, vmem_limit_bytes=24 << 20

time: 13.1 us -> 12.6 us (0.962)
  Pallas kernels: 12.3 us -> 11.8 us
    pallas_call x1, Pallas kernels: 11.2 us -> 10.7 us  [local(): pl.pallas_call(functools.partial(exchange_kernel, tun_size, sec_size), ou...]
where the time goes in v4:
time: 12.6 us; the launch traced here: 12.5 us
  Pallas kernels  11.8 us (94%)
  between operations  0.64 us (5%)
    pallas_call x1, Pallas kernels, local(): pl.pallas_call(functools.partial(exchange_kernel, tun_size, sec_size), ou...  10.7 us
    pallas_call x1, Pallas kernels, local(): pl.pallas_call(output_kernel, out_shape=(jax.ShapeDtypeStruct((3, X, Y, Z...  1.13 us

profile of v4, /device:TPU:12, one launch (start us, length us, event | category | flops | bytes accessed | tf_op | source)
XLA Modules:
  0.0 12.5 jit_solution(406765177405960975)
XLA Ops:
  0.6 10.7 %fields.1 = (f32[5,8,16,128]{3,2,1,0:T(8,128)S(1)}, f32[16,8,16,128]{3,2,1,0:T(8,128)S(1)}, s32[8,16,128]{2,1,0:T(8,128)S(1)}) custom-call(f32[3,8,16,128]{3,2,1,0:T(8,128)} %wind_hbm.1, f32[8,16,128]{2,1,0:T(8,128)} %heat_hbm.1, f32[8,16,128]{2,1,0:T(8,128)} %soot_hbm.1, f32[16,8,16,128]{3,2,1,0:T(8,128)} %mass_hbm.1, s32[8,16,128]{2,1,0:T(8,128)} %count_hbm.1, ...), custom_call_target="tpu_custom_call" | custom-call | tf_op jit(solution)/shard_map/fields/pallas_call | solution.py:371
  11.4 1.1 %outputs.1 = (f32[3,8,16,128]{3,2,1,0:T(8,128)}, f32[8,16,128]{2,1,0:T(8,128)}, f32[8,16,128]{2,1,0:T(8,128)}, f32[16,8,16,128]{3,2,1,0:T(8,128)}, s32[8,16,128]{2,1,0:T(8,128)}) custom-call(f32[5,8,16,128]{3,2,1,0:T(8,128)S(1)} %get-tuple-element.8.state, f32[16,8,16,128]{3,2,1,0:T(8,128)S(1)} %get-tuple-element.9.mass, ...), custom_call_target="tpu_custom_call" | custom-call | tf_op jit(solution)/shard_map/outputs/pallas_call | solution.py:407

commit v5 on v4

--- a/solution.py
+++ b/solution.py
@@ -71,7 +71,7 @@
 
 
 def exchange_kernel(
-    tun_size, sec_size,
+    tun_size, sec_size, parts,
     wind_hbm, heat_hbm, soot_hbm, mass_hbm, count_hbm, label_hbm, onset_hbm,
     state, fresh_mass, tally_out,
     ext, first, kept_first, spray_next, mass, count, label, onset, coef, mass_in,
@@ -201,10 +201,15 @@
     drops = [
         send(6, 1, 0, ext.at[LOAD:SPRAY, X:X + 2, 0:Y], ext.at[LOAD:SPRAY, 0:2, 0:Y]),
         send(7, 1, 0, ext.at[SPRAY, X + 1, 0:Y], ext.at[SPRAY, 1, 0:Y]),
-        send(17, -1, 0, ext.at[SPRAY, 2, 0:Y], ext.at[SPRAY, X + 2, 0:Y]),
+        send(16, -1, 0, ext.at[SPRAY, 2, 0:Y], ext.at[SPRAY, X + 2, 0:Y]),
     ]
     start(drops)
-    masses = [send(16, 1, 0, mass_hbm.at[:, X - 2:X], mass_in)]
+    group = slots // parts
+    masses = [
+        send(17 + i, 1, 0, mass.at[i * group:(i + 1) * group, X - 2:X],
+             mass_in.at[i * group:(i + 1) * group])
+        for i in range(parts)
+    ]
     start(masses)
 
     pack(1)
@@ -305,8 +310,8 @@
         tally_out[x] = n
         return keep, add, n, th, th_ahead
 
-    def slot_masses(x, keep, add, n, source, plane):
-        for k in range(slots):
+    def slot_masses(x, keep, add, n, source, plane, which=range(slots)):
+        for k in which:
             m = source[k, plane]
             fresh_mass[k, x] = jnp.where(n > k, keep * m + add, m)
 
@@ -337,9 +342,11 @@
         first[:, 0] = jnp.zeros((FIELDS + 1, Y + 8, Z), jnp.float32)
 
     lax.fori_loop(1, 3, lowest, (jnp.tanh(first[3, 0]), jnp.tanh(first[3, 1])), unroll=2)
-    wait_recv(masses)
-    for x in range(2):
-        slot_masses(x, coef[0, x], coef[1, x], tally_out[x], mass_in, x)
+    for i in range(parts):
+        wait_recv(masses[i:i + 1])
+        for x in range(2):
+            slot_masses(x, coef[0, x], coef[1, x], tally_out[x], mass_in, x,
+                        range(i * group, (i + 1) * group))
     for a, b, copy in rows_first + fields + drops + across + masses:
         @pl.when(exists(a, b))
         def _(copy=copy):
@@ -366,10 +373,11 @@
 def local(tun_size, sec_size, wind, heat, soot, mass, count, label, onset):
     slots, X, Y, Z = mass.shape
     f32 = jnp.float32
+    parts = 4 if slots % 4 == 0 else 1
     any_spec = pl.BlockSpec(memory_space=pl.ANY)
     vmem_spec = pl.BlockSpec(memory_space=pltpu.VMEM)
     state, fresh_mass, tally = pl.pallas_call(
-        functools.partial(exchange_kernel, tun_size, sec_size),
+        functools.partial(exchange_kernel, tun_size, sec_size, parts),
         out_shape=(
             jax.ShapeDtypeStruct((FIELDS, X, Y, Z), f32),
             jax.ShapeDtypeStruct((slots, X, Y, Z), f32),
@@ -393,8 +401,8 @@
             pltpu.VMEM((2, X + 2, 8, Z), f32),
             pltpu.VMEM((2, X + 2, 8, Z), f32),
             pltpu.SemaphoreType.DMA((7,)),
-            pltpu.SemaphoreType.DMA((18,)),
-            pltpu.SemaphoreType.DMA((18,)),
+            pltpu.SemaphoreType.DMA((17 + parts,)),
+            pltpu.SemaphoreType.DMA((17 + parts,)),
         ],
         compiler_params=pltpu.CompilerParams(
             collective_id=0, has_side_effects=True, vmem_limit_bytes=24 << 20

time: 12.6 us -> 12.7 us (level)
  no operation moved by 1% of the time
where the time goes in v5:
time: 12.7 us; the launch traced here: 12.5 us
  Pallas kernels  11.9 us (94%)
  between operations  0.64 us (5%)
    pallas_call x1, Pallas kernels, local(): pl.pallas_call(functools.partial(exchange_kernel, tun_size, sec_size, par...  10.8 us
    pallas_call x1, Pallas kernels, local(): pl.pallas_call(output_kernel, out_shape=(jax.ShapeDtypeStruct((3, X, Y, Z...  1.13 us

profile of v5, /device:TPU:12, one launch (start us, length us, event | category | flops | bytes accessed | tf_op | source)
XLA Modules:
  0.0 12.5 jit_solution(2552134547545469067)
XLA Ops:
  0.6 10.8 %fields.1 = (f32[5,8,16,128]{3,2,1,0:T(8,128)S(1)}, f32[16,8,16,128]{3,2,1,0:T(8,128)S(1)}, s32[8,16,128]{2,1,0:T(8,128)S(1)}) custom-call(f32[3,8,16,128]{3,2,1,0:T(8,128)} %wind_hbm.1, f32[8,16,128]{2,1,0:T(8,128)} %heat_hbm.1, f32[8,16,128]{2,1,0:T(8,128)} %soot_hbm.1, f32[16,8,16,128]{3,2,1,0:T(8,128)} %mass_hbm.1, s32[8,16,128]{2,1,0:T(8,128)} %count_hbm.1, ...), custom_call_target="tpu_custom_call" | custom-call | tf_op jit(solution)/shard_map/fields/pallas_call | solution.py:379
  11.4 1.1 %outputs.1 = (f32[3,8,16,128]{3,2,1,0:T(8,128)}, f32[8,16,128]{2,1,0:T(8,128)}, f32[8,16,128]{2,1,0:T(8,128)}, f32[16,8,16,128]{3,2,1,0:T(8,128)}, s32[8,16,128]{2,1,0:T(8,128)}) custom-call(f32[5,8,16,128]{3,2,1,0:T(8,128)S(1)} %get-tuple-element.8.state, f32[16,8,16,128]{3,2,1,0:T(8,128)S(1)} %get-tuple-element.9.mass, ...), custom_call_target="tpu_custom_call" | custom-call | tf_op jit(solution)/shard_map/outputs/pallas_call | solution.py:415

commit v6 on v5

--- a/solution.py
+++ b/solution.py
@@ -71,10 +71,10 @@
 
 
 def exchange_kernel(
-    tun_size, sec_size, parts,
+    tun_size, sec_size, parts, detour,
     wind_hbm, heat_hbm, soot_hbm, mass_hbm, count_hbm, label_hbm, onset_hbm,
     state, fresh_mass, tally_out,
-    ext, first, kept_first, spray_next, mass, count, label, onset, coef, mass_in,
+    ext, first, kept_first, spray_next, mass, count, label, onset, coef, mass_in, passing,
     pack_low, pack_high, from_low, from_high,
     local_sem, send_sem, recv_sem,
 ):
@@ -137,9 +137,20 @@
 
         lax.fori_loop(0, X, one, 0, unroll=2)
 
+    for at, to in ((0, 3), (3, 0), (3, 1), (1, 3)):
+        @pl.when(t == detour + at)
+        def _(distance=to - at):
+            pl.semaphore_signal(
+                barrier, inc=1, device_id={"tun": t + distance, "sec": s}, device_id_type=MESH
+            )
+    greeted = (
+        (t == detour).astype(jnp.int32)
+        + (t == detour + 1).astype(jnp.int32)
+        + 2 * (t == detour + 3).astype(jnp.int32)
+    )
     wide = has[-1].astype(jnp.int32) + has[1].astype(jnp.int32)
     deep = has_sec[-1].astype(jnp.int32) + has_sec[1].astype(jnp.int32)
-    pl.semaphore_wait(barrier, (1 + wide) * (1 + deep) - 1)
+    pl.semaphore_wait(barrier, (1 + wide) * (1 + deep) - 1 + greeted)
 
     def send(i, a, b, src, dst):
         return (a, b, pltpu.make_async_remote_copy(
@@ -210,7 +221,24 @@
              mass_in.at[i * group:(i + 1) * group])
         for i in range(parts)
     ]
-    start(masses)
+    start(masses[:1])
+
+    def across_to(i, distance, src, dst):
+        return pltpu.make_async_remote_copy(
+            src_ref=src, dst_ref=dst, send_sem=send_sem.at[i], recv_sem=recv_sem.at[i],
+            device_id={"tun": t + distance, "sec": s}, device_id_type=MESH,
+        )
+
+    outward = across_to(17 + parts, 3, mass.at[group:, X - 2:X], passing)
+    onward = across_to(18 + parts, -2, passing, mass_in.at[group:])
+
+    @pl.when(jnp.logical_and(has[1], t != detour))
+    def _():
+        masses[1][2].start()
+
+    @pl.when(t == detour)
+    def _():
+        outward.start()
 
     pack(1)
     across = [
@@ -327,6 +355,11 @@
 
     first_planes(3, X + 3)
 
+    @pl.when(t == detour + 3)
+    def _():
+        outward.wait_recv()
+        onward.start()
+
     @pl.when(jnp.logical_not(has[1]))
     def _():
         first[:, X + 1] = jnp.zeros((FIELDS + 1, Y + 8, Z), jnp.float32)
@@ -343,14 +376,35 @@
 
     lax.fori_loop(1, 3, lowest, (jnp.tanh(first[3, 0]), jnp.tanh(first[3, 1])), unroll=2)
     for i in range(parts):
-        wait_recv(masses[i:i + 1])
+        if i == 0:
+            wait_recv(masses[:1])
+        else:
+            @pl.when(jnp.logical_and(has[-1], t != detour + 1))
+            def _():
+                masses[1][2].wait_recv()
+
+            @pl.when(t == detour + 1)
+            def _():
+                onward.wait_recv()
         for x in range(2):
             slot_masses(x, coef[0, x], coef[1, x], tally_out[x], mass_in, x,
                         range(i * group, (i + 1) * group))
-    for a, b, copy in rows_first + fields + drops + across + masses:
+    for a, b, copy in rows_first + fields + drops + across + masses[:1]:
         @pl.when(exists(a, b))
         def _(copy=copy):
             copy.wait_send()
+
+    @pl.when(jnp.logical_and(has[1], t != detour))
+    def _():
+        masses[1][2].wait_send()
+
+    @pl.when(t == detour)
+    def _():
+        outward.wait_send()
+
+    @pl.when(t == detour + 3)
+    def _():
+        onward.wait_send()
 
 
 def output_kernel(state, mass, tally, wind_out, heat_out, soot_out, mass_out, count_out, sem):
@@ -373,11 +427,12 @@
 def local(tun_size, sec_size, wind, heat, soot, mass, count, label, onset):
     slots, X, Y, Z = mass.shape
     f32 = jnp.float32
-    parts = 4 if slots % 4 == 0 else 1
+    detour = 3 if tun_size == 8 else -8
+    parts = 2
     any_spec = pl.BlockSpec(memory_space=pl.ANY)
     vmem_spec = pl.BlockSpec(memory_space=pltpu.VMEM)
     state, fresh_mass, tally = pl.pallas_call(
-        functools.partial(exchange_kernel, tun_size, sec_size, parts),
+        functools.partial(exchange_kernel, tun_size, sec_size, parts, detour),
         out_shape=(
             jax.ShapeDtypeStruct((FIELDS, X, Y, Z), f32),
             jax.ShapeDtypeStruct((slots, X, Y, Z), f32),
@@ -396,13 +451,14 @@
             pltpu.SMEM(onset.shape, jnp.int32),
             pltpu.VMEM((2, 2, Y, Z), f32),
             pltpu.VMEM((slots, 2, Y, Z), f32),
+            pltpu.VMEM((slots // 2, 2, Y, Z), f32),
             pltpu.VMEM((2, X, 8, Z), f32),
             pltpu.VMEM((2, X, 8, Z), f32),
             pltpu.VMEM((2, X + 2, 8, Z), f32),
             pltpu.VMEM((2, X + 2, 8, Z), f32),
             pltpu.SemaphoreType.DMA((7,)),
-            pltpu.SemaphoreType.DMA((17 + parts,)),
-            pltpu.SemaphoreType.DMA((17 + parts,)),
+            pltpu.SemaphoreType.DMA((19 + parts,)),
+            pltpu.SemaphoreType.DMA((19 + parts,)),
         ],
         compiler_params=pltpu.CompilerParams(
             collective_id=0, has_side_effects=True, vmem_limit_bytes=24 << 20

time: 12.7 us -> 13.3 us (1.047)
  Pallas kernels: 11.9 us -> 12.5 us
    pallas_call x1, Pallas kernels: 10.8 us -> 11.3 us  [local(): pl.pallas_call(functools.partial(exchange_kernel, tun_size, sec_size, par...]
where the time goes in v6:
time: 13.3 us; the launch traced here: 13.1 us
  Pallas kernels  12.5 us (94%)
  between operations  0.64 us (5%)
    pallas_call x1, Pallas kernels, local(): pl.pallas_call(functools.partial(exchange_kernel, tun_size, sec_size, par...  11.3 us
    pallas_call x1, Pallas kernels, local(): pl.pallas_call(output_kernel, out_shape=(jax.ShapeDtypeStruct((3, X, Y, Z...  1.13 us

profile of v6, /device:TPU:12, one launch (start us, length us, event | category | flops | bytes accessed | tf_op | source)
XLA Modules:
  0.0 13.1 jit_solution(7375117497975248112)
XLA Ops:
  0.6 11.3 %fields.1 = (f32[5,8,16,128]{3,2,1,0:T(8,128)S(1)}, f32[16,8,16,128]{3,2,1,0:T(8,128)S(1)}, s32[8,16,128]{2,1,0:T(8,128)S(1)}) custom-call(f32[3,8,16,128]{3,2,1,0:T(8,128)} %wind_hbm.1, f32[8,16,128]{2,1,0:T(8,128)} %heat_hbm.1, f32[8,16,128]{2,1,0:T(8,128)} %soot_hbm.1, f32[16,8,16,128]{3,2,1,0:T(8,128)} %mass_hbm.1, s32[8,16,128]{2,1,0:T(8,128)} %count_hbm.1, ...), custom_call_target="tpu_custom_call" | custom-call | tf_op jit(solution)/shard_map/fields/pallas_call | solution.py:434
  12.0 1.1 %outputs.1 = (f32[3,8,16,128]{3,2,1,0:T(8,128)}, f32[8,16,128]{2,1,0:T(8,128)}, f32[8,16,128]{2,1,0:T(8,128)}, f32[16,8,16,128]{3,2,1,0:T(8,128)}, s32[8,16,128]{2,1,0:T(8,128)}) custom-call(f32[5,8,16,128]{3,2,1,0:T(8,128)S(1)} %get-tuple-element.8.state, f32[16,8,16,128]{3,2,1,0:T(8,128)S(1)} %get-tuple-element.9.mass, ...), custom_call_target="tpu_custom_call" | custom-call | tf_op jit(solution)/shard_map/outputs/pallas_call | solution.py:471

commit v7 on v5

--- a/solution.py
+++ b/solution.py
@@ -168,6 +168,13 @@
         send(5, -1, 0, soot_hbm.at[0:2], ext.at[4, X + 2:X + 4, 0:Y]),
     ]
     start(fields)
+    group = slots // parts
+    masses = [
+        send(17 + i, 1, 0, mass_hbm.at[i * group:(i + 1) * group, X - 2:X],
+             mass_in.at[i * group:(i + 1) * group])
+        for i in range(parts)
+    ]
+    start(masses[:1])
 
     for c in loads[:3]:
         c.wait()
@@ -204,13 +211,7 @@
         send(16, -1, 0, ext.at[SPRAY, 2, 0:Y], ext.at[SPRAY, X + 2, 0:Y]),
     ]
     start(drops)
-    group = slots // parts
-    masses = [
-        send(17 + i, 1, 0, mass.at[i * group:(i + 1) * group, X - 2:X],
-             mass_in.at[i * group:(i + 1) * group])
-        for i in range(parts)
-    ]
-    start(masses)
+    start(masses[1:])
 
     pack(1)
     across = [

time: 12.7 us -> 12.7 us (level)
  no operation moved by 1% of the time
where the time goes in v7:
time: 12.7 us; the launch traced here: 12.5 us
  Pallas kernels  11.9 us (94%)
  between operations  0.64 us (5%)
    pallas_call x1, Pallas kernels, local(): pl.pallas_call(functools.partial(exchange_kernel, tun_size, sec_size, par...  10.8 us
    pallas_call x1, Pallas kernels, local(): pl.pallas_call(output_kernel, out_shape=(jax.ShapeDtypeStruct((3, X, Y, Z...  1.13 us

profile of v7, /device:TPU:12, one launch (start us, length us, event | category | flops | bytes accessed | tf_op | source)
XLA Modules:
  0.0 12.5 jit_solution(11847221718733802139)
XLA Ops:
  0.6 10.8 %fields.1 = (f32[5,8,16,128]{3,2,1,0:T(8,128)S(1)}, f32[16,8,16,128]{3,2,1,0:T(8,128)S(1)}, s32[8,16,128]{2,1,0:T(8,128)S(1)}) custom-call(f32[3,8,16,128]{3,2,1,0:T(8,128)} %wind_hbm.1, f32[8,16,128]{2,1,0:T(8,128)} %heat_hbm.1, f32[8,16,128]{2,1,0:T(8,128)} %soot_hbm.1, f32[16,8,16,128]{3,2,1,0:T(8,128)} %mass_hbm.1, s32[8,16,128]{2,1,0:T(8,128)} %count_hbm.1, ...), custom_call_target="tpu_custom_call" | custom-call | tf_op jit(solution)/shard_map/fields/pallas_call | solution.py:380
  11.4 1.1 %outputs.1 = (f32[3,8,16,128]{3,2,1,0:T(8,128)}, f32[8,16,128]{2,1,0:T(8,128)}, f32[8,16,128]{2,1,0:T(8,128)}, f32[16,8,16,128]{3,2,1,0:T(8,128)}, s32[8,16,128]{2,1,0:T(8,128)}) custom-call(f32[5,8,16,128]{3,2,1,0:T(8,128)S(1)} %get-tuple-element.8.state, f32[16,8,16,128]{3,2,1,0:T(8,128)S(1)} %get-tuple-element.9.mass, ...), custom_call_target="tpu_custom_call" | custom-call | tf_op jit(solution)/shard_map/outputs/pallas_call | solution.py:416
